TPU v7x, 128 devices: a whole 4x4x4 slice. The times are simulated.
128 devices in a mesh: row: 16 (over x, y), col: 8 (over z, core).
Axes of the slice: x: 4, y: 4, z: 4, core: 2. Of those that a mesh axis runs over, the one named last changes fastest.
Arguments:
- object_slab: float32 [4, 4096, 4096], P(None, 'row', 'col'), may hold values from -6 to 6
- probe_wave: float32 [2, 256, 256], replicated, may hold values from -6 to 6
- scan_offsets: int32 [1024, 2], P(('row', 'col')), may hold values from 0 to 3840, as said below
- live_counts: int32 [128], P(('row', 'col')), may hold values from 1 to 8, as said below
- amplitudes: float32 [1024, 256, 256], P(('row', 'col')), may hold values from 0 to 3
Outputs:
- object_grad: float32 [4, 4096, 4096], P(None, 'row', 'col')
- probe_grad: float32 [2, 256, 256], replicated
Inputs may be any that keep to these rules, and one draw needn't show every extreme that they name: `scan_offsets`: each slot's window lies inside the object, and its corner lies in the object tile of the device that holds the slot. Slot 0 of the first device has corner (0, 0), slot 0 of the last device has corner (3840, 3840). `live_counts`: every device has at least one live slot and some device has all 8 slots live.
All inputs are finite; a program needn't handle non-finite values.
Results may differ from a plain program's by a relative error of at most 0.0003.
Values sent between devices are 32-bit elements; how exact they have to be, the bound alone decides.
No kernel may reach another device: no remote copies, remote signals or barrier semaphores. Data moves between devices by JAX's collectives and lax.ppermute only.
A program may use at most 128 MiB of HBM per device.

v0:
```python
import math

import jax
import jax.numpy as jnp
import ml_dtypes
import numpy as np
from jax import lax
from jax.experimental import pallas as pl
from jax.experimental.pallas import tpu as pltpu
from jax.sharding import PartitionSpec as P

W = 256
HALF_W = 128
TC = 512
EXT = TC + W
SLOTS = 8
GROUP = 4
PREPARED = 2
ADDED = 2
CHUNK = 32
F32 = jnp.float32
BF16 = jnp.bfloat16

RE, IM, NEG_IM = 0, 1, 2


def split_host(table):
    high = table.astype(np.float32).astype(ml_dtypes.bfloat16)
    low = (table - high.astype(np.float64)).astype(np.float32).astype(ml_dtypes.bfloat16)
    return [high, low]


def hop_tables():
    index = np.arange(W)
    dft = np.exp(-2j * np.pi / W * (index[:, None] * index[None, :] % W)) / math.sqrt(W)
    freqs = np.where(index < W // 2, index, index - W) / W
    fresnel = np.exp(-1j * np.pi * (W / 4.0) * freqs**2)
    hop = np.conj(dft) @ (fresnel[:, None] * dft)
    hop = hop * np.exp(1j * np.pi * index / W)
    out = []
    for table in (hop, hop.T):
        for part in (table.real, table.imag, -table.imag):
            out.extend(split_host(part))
    return np.stack(out)


def dft_tables():
    index = np.arange(W)
    angles = 2.0 * np.pi / W * (index[:, None] + 0.5) * (index[None, :HALF_W] + 0.5)
    table = np.concatenate([np.cos(angles), np.sin(angles)], axis=1) / math.sqrt(W)
    return np.stack(split_host(table) + split_host(table.T))


def fold_tables():
    source = np.concatenate([np.arange(HALF_W), np.arange(W - 1, HALF_W - 1, -1)])
    table = np.zeros((W, W), np.float32)
    table[source, np.arange(W)] = 1.0
    return np.stack([table, table.T]).astype(ml_dtypes.bfloat16)


def split(x):
    high = x.astype(BF16)
    return high, (x - high.astype(F32)).astype(BF16)


def lanes(*parts):
    return jnp.concatenate(parts, axis=1)


def rows(*parts):
    return jnp.concatenate(parts, axis=0)


def dot(a, b):
    return jnp.dot(a, b, preferred_element_type=F32)


def half_right(field, tab, at):
    high, low = tab[2 * at], tab[2 * at + 1]
    rh, rl = split(field[0])
    ih, il = split(field[1])
    out = dot(rows(lanes(rh, rl, rh), lanes(ih, il, ih)), rows(high, high, low))
    return out[:W], out[W:]


def half_left(field, tab, at):
    high, low = tab[2 * at], tab[2 * at + 1]
    rh, rl = split(field[0])
    ih, il = split(field[1])
    out = dot(lanes(high, high, low), lanes(rows(rh, rl, rh), rows(ih, il, ih)))
    return out[:, :W], out[:, W:]


def hop_parts(tab, at, conj):
    im, neg = (IM, NEG_IM) if not conj else (NEG_IM, IM)

    def three(a, b):
        a, b = 2 * (3 * at + a), 2 * (3 * at + b)
        return [tab[a], tab[b], tab[a], tab[b], tab[a + 1], tab[b + 1]]

    return three(RE, neg), three(im, RE)


def hop_right(field, tab, at, conj):
    rh, rl = split(field[0])
    ih, il = split(field[1])
    to_re, to_im = hop_parts(tab, at, conj)
    out = dot(lanes(rh, ih, rl, il, rh, ih), lanes(rows(*to_re), rows(*to_im)))
    return out[:, :W], out[:, W:]


def hop_left(field, tab, at, conj):
    rh, rl = split(field[0])
    ih, il = split(field[1])
    to_re, to_im = hop_parts(tab, at, conj)
    out = dot(rows(lanes(*to_re), lanes(*to_im)), rows(rh, ih, rl, il, rh, ih))
    return out[:W], out[W:]


def spread_right(field):
    c, s = field[0][:, :HALF_W], field[0][:, HALF_W:]
    d, t = field[1][:, :HALF_W], field[1][:, HALF_W:]
    return lanes(c + t, t - c), lanes(d - s, -d - s)


def spread_left(field):
    c, s = field[0][:HALF_W], field[0][HALF_W:]
    d, t = field[1][:HALF_W], field[1][HALF_W:]
    return rows(c + t, t - c), rows(d - s, -d - s)


def gather_right(field):
    a, b = field[0][:, :HALF_W], field[0][:, HALF_W:]
    c, d = field[1][:, :HALF_W], field[1][:, HALF_W:]
    return lanes(a - b, -c - d), lanes(c - d, a + b)


def gather_left(field):
    a, b = field[0][:HALF_W], field[0][HALF_W:]
    c, d = field[1][:HALF_W], field[1][HALF_W:]
    return rows(a - b, -c - d), rows(c - d, a + b)


def times(a, b):
    return a[0] * b[0] - a[1] * b[1], a[0] * b[1] + a[1] * b[0]


def conj_times(a, b):
    return a[0] * b[0] + a[1] * b[1], a[0] * b[1] - a[1] * b[0]


def pair(ref, *at):
    return ref[(*at, 0)], ref[(*at, 1)]


def put(value, ref, *at):
    ref[(*at, 0)], ref[(*at, 1)] = value


def chunks(body):
    def step(i, carry):
        body(pl.multiple_of(i * CHUNK, CHUNK))
        return carry

    lax.fori_loop(0, W // CHUNK, step, 0)


def geometry(meta, slot):
    row, col = meta[1 + slot], meta[1 + SLOTS + slot]
    block = col // W
    first = pl.multiple_of(block * W, W)
    second = pl.multiple_of(block * W + W, W)
    return row, col - block * W, first, second


def masks(row, col, at):
    in_top = lax.broadcasted_iota(jnp.int32, (CHUNK, W), 0) + at >= row
    in_first = lax.broadcasted_iota(jnp.int32, (CHUNK, W), 1) >= col
    return in_top, in_first


def load_window(meta, slot, ext, planes, win, u):
    row, col, first, second = geometry(meta, slot)
    border = row // CHUNK

    def load(i, carry):
        here = pl.ds(pl.multiple_of(i * CHUNK, CHUNK), CHUNK)
        _, in_first = masks(row, col, 0)
        low = (i < border).astype(jnp.int32)
        for p in planes:
            win[u, p, here, :] = jnp.where(
                in_first, ext[low, p, here, pl.ds(first, W)], ext[low, p, here, pl.ds(second, W)]
            )
        return carry

    lax.fori_loop(0, W // CHUNK, load, 0, unroll=True)
    at = pl.multiple_of(border * CHUNK, CHUNK)
    here = pl.ds(at, CHUNK)
    in_top, in_first = masks(row, col, at)
    for p in planes:
        low = jnp.where(in_first, ext[1, p, here, pl.ds(first, W)], ext[1, p, here, pl.ds(second, W)])
        win[u, p, here, :] = jnp.where(in_top, win[u, p, here, :], low)


def add_window(meta, slot, win, u, planes, gext):
    row, col, first, second = geometry(meta, slot)
    border = row // CHUNK
    zero = jnp.zeros((CHUNK, W), F32)
    alive = slot < meta[0]

    def add(i, carry):
        at = pl.multiple_of(i * CHUNK, CHUNK)
        here = pl.ds(at, CHUNK)
        in_top, in_first = masks(row, col, at)
        low = (i < border).astype(jnp.int32)
        keep = jnp.logical_and(jnp.logical_or(in_top, i < border), alive)
        for p in planes:
            value = jnp.where(keep, win[u, p, here, :], zero)
            gext[low, p, here, pl.ds(first, W)] += jnp.where(in_first, value, zero)
            gext[low, p, here, pl.ds(second, W)] += jnp.where(in_first, zero, value)
        return carry

    lax.fori_loop(0, W // CHUNK, add, 0, unroll=True)
    at = pl.multiple_of(border * CHUNK, CHUNK)
    here = pl.ds(at, CHUNK)
    in_top, in_first = masks(row, col, at)
    for p in planes:
        value = jnp.where(jnp.logical_and(jnp.logical_not(in_top), alive), win[u, p, here, :], zero)
        gext[1, p, here, pl.ds(first, W)] += jnp.where(in_first, value, zero)
        gext[1, p, here, pl.ds(second, W)] += jnp.where(in_first, zero, value)


def turn_probe(meta, slot, twice, turned, u):
    row, col, _, _ = geometry(meta, slot)
    for p in range(2):
        here = pl.ds(W - row, W)
        turned[u, p] = pltpu.roll(lanes(twice[p, 0, here, :], twice[p, 1, here, :]), col, 1)


def add_probe(meta, slot, part, u, acc):
    row, col, _, _ = geometry(meta, slot)
    for p in range(2):
        here = pl.ds(W - row, W)
        value = jnp.where(slot < meta[0], pltpu.roll(part[u, p], W - col, 1), 0.0)
        acc[p, 0, here, :] += value[:, :HALF_W]
        acc[p, 1, here, :] += value[:, HALF_W:]


def tile_copies(refs, ext, sems):
    own, right, down0, down1, corner = refs
    return [
        (own, ext.at[0, :, :, pl.ds(0, TC)], sems.at[0]),
        (right, ext.at[0, :, :, pl.ds(TC, W)], sems.at[1]),
        (down0, ext.at[1, :, :, pl.ds(0, W)], sems.at[2]),
        (down1, ext.at[1, :, :, pl.ds(W, W)], sems.at[3]),
        (corner, ext.at[1, :, :, pl.ds(TC, W)], sems.at[4]),
    ]


def start_copies(copies):
    copies = [pltpu.make_async_copy(*copy) for copy in copies]
    for copy in copies:
        copy.start()
    return copies


def wait_copies(copies):
    for copy in copies:
        copy.wait()


def prepare_kernel(meta, probe, amp, fold, amp_out, turned, twice):
    step = pl.program_id(0)

    def fold_amplitudes(u):
        high = amp[u].astype(BF16)
        rest = amp[u] - high.astype(F32)
        mid = rest.astype(BF16)
        low = (rest - mid.astype(F32)).astype(BF16)
        right_way = dot(rows(high, mid, low), fold[0])
        out = dot(fold[1], lanes(*(right_way[i * W : (i + 1) * W].astype(BF16) for i in range(3))))
        amp_out[u] = out[:, :W] + out[:, W : 2 * W] + out[:, 2 * W :]

    @pl.when(step == 0)
    def double_probe():
        for p in range(2):
            for half in range(2):
                part = probe[p, :, half * HALF_W : (half + 1) * HALF_W]
                twice[p, half, :W, :] = part
                twice[p, half, W:, :] = part

    for u in range(PREPARED):
        fold_amplitudes(u)
        turn_probe(meta, step * PREPARED + u, twice, turned, u)


def first_kernel(meta, own, right, down0, down1, corner, turned, tab, prop, ext, win, sems):
    step = pl.program_id(0)

    @pl.when(step == 0)
    def begin():
        one = pl.ds(0, 2)
        refs = (own.at[one], right.at[one], down0, down1, corner)
        wait_copies(start_copies(tile_copies(refs, ext, sems)))

    @pl.when(step * GROUP < meta[0])
    def work():
        for u in range(GROUP):
            load_window(meta, step * GROUP + u, ext, (0, 1), win, u)
        fields = [times(pair(turned, u), pair(win, u)) for u in range(GROUP)]
        fields = [hop_right(f, tab, 0, False) for f in fields]
        fields = [hop_left(f, tab, 1, False) for f in fields]
        for u, f in enumerate(fields):
            put(f, prop, u)


def second_kernel(meta, own, right, down0_one, down0_two, down1_one, corner_one, turned_in, hop_in, prop_in, amp_in,
                  down1_two, corner_two, dft, gprobe, win,
                  ext, acc, turned, hop, prop, amp, sems):
    step = pl.program_id(0)
    group = range(GROUP)
    one, two = pl.ds(0, 2), pl.ds(2, 2)
    refs_one = (own.at[one], right.at[one], down0_one, down1_one, corner_one)
    refs_two = (own.at[two], right.at[two], down0_two, down1_two, corner_two)
    copies_one = tile_copies(refs_one, ext.at[:, one], sems.at[0])
    copies_two = tile_copies(refs_two, ext.at[:, two], sems.at[1])
    now, later = pl.ds(0, GROUP), pl.ds(GROUP, SLOTS - GROUP)
    copies_now = copies_two + [
        (prop_in.at[now], prop.at[now], sems.at[2, 0]),
        (amp_in.at[now], amp.at[now], sems.at[2, 1]),
    ]
    copies_later = [(hop_in, hop, sems.at[2, 2])] + copies_one + [
        (turned_in, turned, sems.at[2, 3]),
        (prop_in.at[later], prop.at[later], sems.at[2, 4]),
        (amp_in.at[later], amp.at[later], sems.at[2, 5]),
    ]

    @pl.when(step == 0)
    def begin():
        started = start_copies(copies_now)
        start_copies(copies_later)
        acc[...] = jnp.zeros_like(acc)
        wait_copies(started)

    live = step * GROUP < meta[0]

    @pl.when(live)
    def stage_one():
        for u in group:
            load_window(meta, step * GROUP + u, ext, (2, 3), win, u)
        fields = [times(pair(prop, step * GROUP + u), (win[u, 2], win[u, 3])) for u in group]
        fields = [spread_left(half_left(f, dft, 1)) for f in fields]
        fields = [spread_right(half_right(f, dft, 0)) for f in fields]
        chi = []
        for u, f in enumerate(fields):
            factor = 1.0 - amp[step * GROUP + u] * lax.rsqrt(f[0] * f[0] + f[1] * f[1] + 1.0)
            chi.append((factor * f[0], factor * f[1]))
        fields = [half_right(gather_right(f), dft, 1) for f in chi]
        fields = [half_left(gather_left(f), dft, 0) for f in fields]
        waves = [conj_times((win[u, 2], win[u, 3]), f) for u, f in enumerate(fields)]
        for u, f in enumerate(fields):
            win[u, 2], win[u, 3] = conj_times(pair(prop, step * GROUP + u), f)
        for u, f in enumerate(waves):
            put(f, prop, step * GROUP + u)

    @pl.when(step == 0)
    def arrive():
        wait_copies([pltpu.make_async_copy(*copy) for copy in copies_later])

    @pl.when(live)
    def stage_two():
        for u in group:
            load_window(meta, step * GROUP + u, ext, (0, 1), win, u)
        waves = [hop_left(pair(prop, step * GROUP + u), hop, 0, True) for u in group]
        waves = [hop_right(f, hop, 1, True) for f in waves]
        for u, wave in enumerate(waves):
            probe = pair(turned, step * GROUP + u)
            grad, part = conj_times(probe, wave), conj_times(pair(win, u), wave)
            put(grad, win, u)
            put(part, prop, step * GROUP + u)

        def finish(slot, u):
            add_probe(meta, slot, prop, slot, acc)

        for u in group:
            slot = step * GROUP + u
            finish(slot, u)

    @pl.when(step == SLOTS // GROUP - 1)
    def end():
        for p in range(2):
            gprobe[p] = lanes(acc[p, 0, :W, :] + acc[p, 0, W:, :], acc[p, 1, :W, :] + acc[p, 1, W:, :])


def third_kernel(meta, grads, gown, gright, gdown0, gdown1, gcorner, gext, sems):
    step = pl.program_id(0)

    @pl.when(step == 0)
    def begin():
        gext[...] = jnp.zeros_like(gext)

    for u in range(ADDED):
        slot = step * ADDED + u
        pl.when(slot < meta[0])(lambda: add_window(meta, slot, grads, u, range(4), gext))

    @pl.when(step == SLOTS // ADDED - 1)
    def end():
        wait_copies(start_copies([
            (gext.at[1, :, :, pl.ds(W, W)], gdown1, sems.at[0]),
            (gext.at[1, :, :, pl.ds(TC, W)], gcorner, sems.at[1]),
            (gext.at[1, :, :, pl.ds(0, W)], gdown0, sems.at[2]),
            (gext.at[0, :, :, pl.ds(TC, W)], gright, sems.at[3]),
            (gext.at[0, :, :, pl.ds(0, TC)], gown, sems.at[4]),
        ]))


ANYWHERE = pl.BlockSpec(memory_space=pl.ANY)
WHOLE = pl.BlockSpec(memory_space=pltpu.VMEM)
SCALARS = pl.BlockSpec(memory_space=pltpu.SMEM)
FIELDS = pl.BlockSpec((GROUP, 2, W, W), lambda i: (i, 0, 0, 0))
PLANES = pl.BlockSpec((GROUP, W, W), lambda i: (i, 0, 0))


def shape(*dims):
    return jax.ShapeDtypeStruct(dims, F32)


FIELDS_SHAPE = shape(SLOTS, 2, W, W)


def call(kernel, steps, in_specs, out_specs, out_shape, scratch, products, mebibytes):
    return pl.pallas_call(
        kernel,
        grid=(steps,),
        in_specs=in_specs,
        out_specs=out_specs,
        out_shape=out_shape,
        scratch_shapes=scratch,
        compiler_params=pltpu.CompilerParams(
            vmem_limit_bytes=mebibytes * 2**20, dimension_semantics=("arbitrary",)
        ),
        cost_estimate=pl.CostEstimate(
            flops=SLOTS * products * 2 * W**3, bytes_accessed=products * 2**18, transcendentals=0
        ),
    )


def prepare_call(*args):
    return call(
        prepare_kernel,
        SLOTS // PREPARED,
        [SCALARS, WHOLE, pl.BlockSpec((PREPARED, W, W), lambda i: (i, 0, 0)), WHOLE],
        [
            pl.BlockSpec((PREPARED, W, W), lambda i: (i, 0, 0)),
            pl.BlockSpec((PREPARED, 2, W, W), lambda i: (i, 0, 0, 0)),
        ],
        [shape(SLOTS, W, W), FIELDS_SHAPE],
        [pltpu.VMEM((2, 2, 2 * W, HALF_W), F32)],
        0,
        16,
    )(*args)


def first_call(*args):
    return call(
        first_kernel,
        SLOTS // GROUP,
        [SCALARS] + [ANYWHERE] * 3 + [WHOLE, WHOLE, FIELDS, WHOLE],
        FIELDS,
        FIELDS_SHAPE,
        [
            pltpu.VMEM((2, 2, W, EXT), F32),
            pltpu.VMEM((GROUP, 2, W, W), F32),
            pltpu.SemaphoreType.DMA((5,)),
        ],
        24,
        52,
    )(*args)


def second_call(*args):
    return call(
        second_kernel,
        SLOTS // GROUP,
        [SCALARS] + [ANYWHERE] * 10 + [WHOLE] * 3,
        [WHOLE, pl.BlockSpec((GROUP, 4, W, W), lambda i: (i, 0, 0, 0))],
        [shape(2, W, W), shape(SLOTS, 4, W, W)],
        [
            pltpu.VMEM((2, 4, W, EXT), F32),
            pltpu.VMEM((2, 2, 2 * W, HALF_W), F32),
            pltpu.VMEM((SLOTS, 2, W, W), F32),
            pltpu.VMEM((12, W, W), BF16),
            pltpu.VMEM((SLOTS, 2, W, W), F32),
            pltpu.VMEM((SLOTS, W, W), F32),
            pltpu.SemaphoreType.DMA((3, 6)),
        ],
        48,
        54,
    )(*args)


def third_call(*args):
    return call(
        third_kernel,
        SLOTS // ADDED,
        [SCALARS, pl.BlockSpec((ADDED, 4, W, W), lambda i: (i, 0, 0, 0))],
        [ANYWHERE] * 5,
        [shape(4, W, TC)] + [shape(4, W, W)] * 4,
        [pltpu.VMEM((2, 4, W, EXT), F32), pltpu.SemaphoreType.DMA((5,))],
        24,
        40,
    )(*args)


def add_kernel(base, right, down0, down1, out):
    first, second = pl.ds(0, W), pl.ds(W, W)
    out[:, :, first] = base[:, :, first] + (right[...] + down0[...])
    out[:, :, second] = base[:, :, second] + down1[...]


def add_call(*args):
    whole = pl.BlockSpec((1, W, TC), lambda i: (i, 0, 0))
    part = pl.BlockSpec((1, W, W), lambda i: (i, 0, 0))
    return pl.pallas_call(
        add_kernel,
        grid=(4,),
        in_specs=[whole] + [part] * 3,
        out_specs=whole,
        out_shape=shape(4, W, TC),
        compiler_params=pltpu.CompilerParams(vmem_limit_bytes=8 * 2**20),
        cost_estimate=pl.CostEstimate(flops=2**20, bytes_accessed=7 * 2**20, transcendentals=0),
    )(*args)


def shift(value, axis, steps):
    count = lax.axis_size(axis)
    first, last = (max(0, -steps), min(count, count - steps))
    return lax.ppermute(value, axis, [(source, source + steps) for source in range(first, last)])


def add_shares(value, axis):
    count = lax.axis_size(axis)
    shares = value.reshape(count, -1, value.shape[-1])
    return lax.all_to_all(shares, axis, 0, 0, tiled=True).sum(axis=0)


def hand_out(value, axis):
    spread = jnp.broadcast_to(value[None], (lax.axis_size(axis), *value.shape))
    return lax.all_to_all(spread, axis, 0, 0, tiled=True)


def ring_sum(value, pairs):
    first = lax.ppermute(value, "row", pairs)
    second = lax.ppermute(first, "row", pairs)
    third = lax.ppermute(second, "row", pairs)
    return (value + second) + (first + third)


def ring_sum_after(value, pairs, arrived):
    first = lax.ppermute(value, "row", pairs)
    second = lax.ppermute(first, "row", pairs)
    second, arrived = lax.optimization_barrier((second, arrived))
    third = lax.ppermute(second, "row", pairs)
    return (value + second) + (first + third), arrived


def body(object_slab, probe_wave, scan_offsets, live_counts, amplitudes):
    rows_tile, cols_tile = object_slab.shape[1:]
    local_rows = scan_offsets[:, 0] - lax.axis_index("row") * rows_tile
    local_cols = scan_offsets[:, 1] - lax.axis_index("col") * cols_tile
    meta = jnp.concatenate([live_counts, local_rows, local_cols])
    hop, dft, fold = jnp.asarray(hop_tables()), jnp.asarray(dft_tables()), jnp.asarray(fold_tables())
    first_part, rest = lax.optimization_barrier((object_slab[:2, :, :W], object_slab))
    down0_one = shift(first_part, "row", -1)
    down1_one = shift(rest[:2, :, W:], "row", -1)
    right = shift(rest[:, :, :W], "col", -1)
    down0_two = shift(rest[2:, :, :W], "row", -1)
    amp, turned = prepare_call(meta, probe_wave, amplitudes, fold)
    down0_one, turned, last_part = lax.optimization_barrier((down0_one, turned, rest[2:, :, W:]))
    corner_one = shift(down0_one, "col", -1)
    down1_two = shift(last_part, "row", -1)
    prop = first_call(meta, object_slab, right, down0_one, down1_one, corner_one, turned, hop)
    down0_two, prop = lax.optimization_barrier((down0_two, prop))
    corner_two = shift(down0_two, "col", -1)
    gprobe, grads = second_call(
        meta, object_slab, right, down0_one, down0_two, down1_one, corner_one, turned, hop, prop, amp,
        down1_two, corner_two, dft,
    )
    share = add_shares(gprobe, "col")
    gown, gright, gdown0, gdown1, gcorner = third_call(meta, grads)
    side = lax.axis_size("row") // 4
    to_left_x = [(i, (i - side) % (4 * side)) for i in range(4 * side)]
    to_left_y = [(i, i - i % side + (i - 1) % side) for i in range(4 * side)]
    gcorner, gright, gdown0, gdown1, share = lax.optimization_barrier((gcorner, gright, gdown0, gdown1, share))
    corner_back = shift(gcorner, "col", 1)
    down1_back = shift(gdown1, "row", 1)
    gdown0 = gdown0 + corner_back
    down0_back = shift(gdown0, "row", 1)
    right_back = shift(gright, "col", 1)
    share, down1_back = ring_sum_after(ring_sum(share, to_left_x), to_left_y, down1_back)
    right_back, share = lax.optimization_barrier((right_back, share))
    probe_grad = hand_out(share, "col").reshape(probe_wave.shape)
    return add_call(gown, right_back, down0_back, down1_back), probe_grad


def solution(mesh):
    return jax.shard_map(
        body,
        mesh=mesh,
        in_specs=(
            P(None, "row", "col"),
            P(),
            P(("row", "col"), None),
            P(("row", "col")),
            P(("row", "col"), None, None),
        ),
        out_specs=(P(None, "row", "col"), P()),
        check_vma=False,
    )
```

profile of v0, /device:TPU:6, one launch (start us, length us, event | category | flops | bytes accessed | tf_op | source)
XLA Modules:
  0.0 153.2 jit_solution(17073841379397048581)
XLA Ops:
  0.6 0.0 copy-start.12
  0.6 2.0 %slice.23 = f32[2,256,256]{2,1,0:T(8,128)} slice(f32[4,256,512]{2,1,0:T(8,128)} %own.3), slice={[0:2], [0:256], [0:256]} | slice | bytes 1048576 | tf_op jit(solution)/shard_map/slice | solution.py:573
  2.7 5.2 %collective-permute-start.1 = (f32[2,256,256]{2,1,0:T(8,128)}, f32[2,256,256]{2,1,0:T(8,128)S(1)}, u32[]{:S(2)}, u32[]{:S(2)}) collective-permute-start(f32[2,256,256]{2,1,0:T(8,128)} %slice.23), channel_id=1, source_target_pairs={{8,0},{16,8},{24,16},{32,24},{40,32},{48,40},{56,48},{64,56},{72,6... | collective-permute-start | bytes 1572872 | tf_op jit(solution)/shard_map/ppermute | solution.py:538
  7.8 2.3 %slice.24 = f32[4,256,256]{2,1,0:T(8,128)} slice(f32[4,256,512]{2,1,0:T(8,128)} %own.3), slice={[0:4], [0:256], [0:256]} | slice | bytes 2097152 | tf_op jit(solution)/shard_map/slice | solution.py:576
  10.1 1.6 %collective-permute-start = (f32[4,256,256]{2,1,0:T(8,128)}, f32[4,256,256]{2,1,0:T(8,128)}, u32[]{:S(2)}, u32[]{:S(2)}) collective-permute-start(f32[4,256,256]{2,1,0:T(8,128)} %slice.24), channel_id=1, source_target_pairs={{1,0},{2,1},{3,2},{4,3},{5,4},{6,5},{7,6},{9,8},{10,9},{11,10},{12... | collective-permute-start | bytes 3145736 | tf_op jit(solution)/shard_map/ppermute | solution.py:538
  11.7 1.2 fusion
  12.9 2.6 %collective-permute-start.3 = (f32[2,256,256]{2,1,0:T(8,128)}, f32[2,256,256]{2,1,0:T(8,128)}, u32[]{:S(2)}, u32[]{:S(2)}) collective-permute-start(f32[2,256,256]{2,1,0:T(8,128)} %get-tuple-element.52), channel_id=1, source_target_pairs={{8,0},{16,8},{24,16},{32,24},{40,32},{48,40},{56,48},{64,56},{72,6... | collective-permute-start | bytes 1572872 | tf_op jit(solution)/shard_map/ppermute | solution.py:538
  16.2 0.1 pad_add_fusion.meta
  16.3 0.0 copy-done.1
  16.3 3.7 %shard_map.95 = (f32[8,256,256]{2,1,0:T(8,128)S(1)}, f32[8,2,256,256]{3,2,1,0:T(8,128)S(1)}) custom-call(s32[17]{0:T(128)S(1)} %pad_add_fusion.meta, f32[2,256,256]{2,1,0:T(8,128)S(1)} %copy-done.1, f32[8,256,256]{2,1,0:T(8,128)S(1)} %copy-done, bf16[2,256,256]{2,1,0:T(8,128)(2,1)S(1)} %copy-done.2), custom_call_target="tpu_custom_call" | custom-call | tf_op jit(solution)/shard_map/pallas_call | solution.py:449
  20.0 2.0 %copy-done.5 = f32[8,2,256,256]{3,2,1,0:T(8,128)} copy-done((f32[8,2,256,256]{3,2,1,0:T(8,128)}, f32[8,2,256,256]{3,2,1,0:T(8,128)S(1)}, u32[]{:S(2)}) %copy-start.5) | copy-done | bytes 4194328
  22.1 1.3 copy-done.6
  23.4 0.0 collective-permute-done.1.down0.down0_one
  23.4 1.3 collective-permute-start.4
  24.7 3.5 %collective-permute-start.2 = (f32[2,256,256]{2,1,0:T(8,128)S(1)}, f32[2,256,256]{2,1,0:T(8,128)S(1)}, u32[]{:S(2)}, u32[]{:S(2)}) collective-permute-start(f32[2,256,256]{2,1,0:T(8,128)S(1)} %copy-done.14), channel_id=1, source_target_pairs={{8,0},{16,8},{24,16},{32,24},{40,32},{48,40},{56,48},{64,56},{72,6... | collective-permute-start | bytes 1572872 | tf_op jit(solution)/shard_map/ppermute | solution.py:538
  28.2 0.0 copy-done.13
  28.2 1.9 %collective-permute-start.5 = (f32[2,256,256]{2,1,0:T(8,128)S(1)}, f32[2,256,256]{2,1,0:T(8,128)S(1)}, u32[]{:S(2)}, u32[]{:S(2)}) collective-permute-start(f32[2,256,256]{2,1,0:T(8,128)S(1)} %copy-done.13), channel_id=1, source_target_pairs={{8,0},{16,8},{24,16},{32,24},{40,32},{48,40},{56,48},{64,56},{72,6... | collective-permute-start | bytes 1572872 | tf_op jit(solution)/shard_map/ppermute | solution.py:538
  30.1 1.4 collective-permute-done.3.down1.down1_one
  31.6 0.0 collective-permute-done.right
  31.6 0.0 collective-permute-done.4.corner.corner_one
  31.6 9.7 %shard_map.96.prop_in = f32[8,2,256,256]{3,2,1,0:T(8,128)} custom-call(s32[17]{0:T(128)S(1)} %pad_add_fusion.meta, f32[4,256,512]{2,1,0:T(8,128)} %own.3, f32[4,256,256]{2,1,0:T(8,128)} %collective-permute-done.right, f32[2,256,256]{2,1,0:T(8,128)S(1)} %collective-permute-done.1.down0.down0_one, f32[2,256,256]{2,1,0:T(8,128)} %collective-permute-done.3.down1.down1_one, ...), custom_call_target="tpu_custom_call" | custom-call | flops 6442450944 | bytes 6291456 | tf_op jit(solution)/shard_map/pallas_call | solution.py:465
  41.3 0.0 copy-done.3
  41.3 0.0 copy-done.10
  41.3 0.0 copy-done.11
  41.3 1.4 collective-permute-done.2.down0_two
  42.7 1.5 collective-permute-start.6
  44.2 8.8 %collective-permute-done.5.down1_two = f32[2,256,256]{2,1,0:T(8,128)S(1)} collective-permute-done((f32[2,256,256]{2,1,0:T(8,128)S(1)}, f32[2,256,256]{2,1,0:T(8,128)S(1)}, u32[]{:S(2)}, u32[]{:S(2)}) %collective-permute-start.5) | collective-permute-done | bytes 524320 | tf_op jit(solution)/shard_map/ppermute | solution.py:538
  52.9 0.0 collective-permute-done.6.corner_two
  52.9 0.8 copy-done.17
  53.7 0.2 copy-done.18
  53.9 15.7 %shard_map.97 = (f32[2,256,256]{2,1,0:T(8,128)}, f32[8,4,256,256]{3,2,1,0:T(8,128)}) custom-call(s32[17]{0:T(128)} %copy-done.3, f32[4,256,512]{2,1,0:T(8,128)} %own.3, f32[4,256,256]{2,1,0:T(8,128)} %collective-permute-done.right, f32[2,256,256]{2,1,0:T(8,128)} %copy-done.10, f32[2,256,256]{2,1,0:T(8,128)} %copy-done.16, ...), custom_call_target="tpu_custom_call" | custom-call | flops 12884901888 | bytes 12582912 | tf_op jit(solution)/shard_map/pallas_call | solution.py:482
  69.6 13.8 %all-to-all-start = ((f32[8,64,256]{2,1,0:T(8,128)}), f32[8,64,256]{2,1,0:T(8,128)}, u32[]{:S(2)}, u32[]{:S(2)}) async-start(f32[8,64,256]{2,1,0:T(8,128)} %bitcast.7), calls=%async_computation | async-start | bytes 1048576 | tf_op jit(solution)/shard_map/all_to_all | solution.py:544
  83.4 0.0 copy-done.4
  83.4 5.9 %shard_map.98 = (f32[4,256,512]{2,1,0:T(8,128)S(1)}, f32[4,256,256]{2,1,0:T(8,128)S(1)}, f32[4,256,256]{2,1,0:T(8,128)S(1)}, f32[4,256,256]{2,1,0:T(8,128)S(1)}, f32[4,256,256]{2,1,0:T(8,128)S(1)}) custom-call(s32[17]{0:T(128)S(1)} %copy-done.4, f32[8,4,256,256]{3,2,1,0:T(8,128)} %get-tuple-element.36.grads), custom_call_target="tpu_custom_call" | custom-call | flops 6442450944 | bytes 6291456 | tf_op jit(solution)/shard_map/pallas_call | solution.py:503
  89.3 0.0 copy-start.7
  89.3 1.0 copy-done.7
  90.3 1.0 copy-done.8
  91.3 1.0 copy-done.9
  92.2 1.6 %all-to-all-done = f32[8,64,256]{2,1,0:T(8,128)} async-done(((f32[8,64,256]{2,1,0:T(8,128)}), f32[8,64,256]{2,1,0:T(8,128)}, u32[]{:S(2)}, u32[]{:S(2)}) %all-to-all-start) | async-done | bytes 524320 | tf_op jit(solution)/shard_map/all_to_all | solution.py:544
  93.8 1.1 reduce_sum.9
  94.9 3.9 %collective-permute-start.15 = (f32[4,256,256]{2,1,0:T(8,128)}, f32[4,256,256]{2,1,0:T(8,128)S(1)}, u32[]{:S(2)}, u32[]{:S(2)}) collective-permute-start(f32[4,256,256]{2,1,0:T(8,128)} %copy-done.9), channel_id=1, source_target_pairs={{0,1},{1,2},{2,3},{3,4},{4,5},{5,6},{6,7},{8,9},{9,10},{10,11},{11... | collective-permute-start | bytes 3145736 | tf_op jit(solution)/shard_map/ppermute | solution.py:538
  98.8 3.1 %collective-permute-start.13 = (f32[4,256,256]{2,1,0:T(8,128)}, f32[4,256,256]{2,1,0:T(8,128)S(1)}, u32[]{:S(2)}, u32[]{:S(2)}) collective-permute-start(f32[4,256,256]{2,1,0:T(8,128)} %copy-done.8), channel_id=1, source_target_pairs={{0,8},{8,16},{16,24},{24,32},{32,40},{40,48},{48,56},{56,64},{64,7... | collective-permute-start | bytes 3145736 | tf_op jit(solution)/shard_map/ppermute | solution.py:538
  102.0 1.6 %collective-permute-start.7 = (f32[4,256,256]{2,1,0:T(8,128)}, f32[4,256,256]{2,1,0:T(8,128)S(1)}, u32[]{:S(2)}, u32[]{:S(2)}) collective-permute-start(f32[4,256,256]{2,1,0:T(8,128)} %copy-done.7), channel_id=1, source_target_pairs={{0,1},{1,2},{2,3},{3,4},{4,5},{5,6},{6,7},{8,9},{9,10},{10,11},{11... | collective-permute-start | bytes 3145736 | tf_op jit(solution)/shard_map/ppermute | solution.py:538
  103.6 0.6 collective-permute-start.8
  104.3 4.9 %collective-permute-done.8 = f32[64,256]{1,0:T(8,128)S(1)} collective-permute-done((f32[64,256]{1,0:T(8,128)S(1)}, f32[64,256]{1,0:T(8,128)S(1)}, u32[]{:S(2)}, u32[]{:S(2)}) %collective-permute-start.8) | collective-permute-done | bytes 65568 | tf_op jit(solution)/shard_map/ppermute | solution.py:553
  109.2 0.0 collective-permute-start.9
  109.2 5.5 %collective-permute-done.9 = f32[64,256]{1,0:T(8,128)S(1)} collective-permute-done((f32[64,256]{1,0:T(8,128)S(1)}, f32[64,256]{1,0:T(8,128)S(1)}, u32[]{:S(2)}, u32[]{:S(2)}) %collective-permute-start.9) | collective-permute-done | bytes 65568 | tf_op jit(solution)/shard_map/ppermute | solution.py:554
  114.7 0.0 collective-permute-start.10
  114.7 0.0 collective-permute-done.15
  114.7 0.1 add.27
  114.8 2.2 %collective-permute-start.16 = (f32[4,256,256]{2,1,0:T(8,128)S(1)}, f32[4,256,256]{2,1,0:T(8,128)S(1)}, u32[]{:S(2)}, u32[]{:S(2)}) collective-permute-start(f32[4,256,256]{2,1,0:T(8,128)S(1)} %add.27), channel_id=1, source_target_pairs={{0,8},{8,16},{16,24},{24,32},{32,40},{40,48},{48,56},{56,64},{64,7... | collective-permute-start | bytes 3145736 | tf_op jit(solution)/shard_map/ppermute | solution.py:538
  117.0 3.1 %collective-permute-done.10 = f32[64,256]{1,0:T(8,128)S(1)} collective-permute-done((f32[64,256]{1,0:T(8,128)S(1)}, f32[64,256]{1,0:T(8,128)S(1)}, u32[]{:S(2)}, u32[]{:S(2)}) %collective-permute-start.10) | collective-permute-done | bytes 65568 | tf_op jit(solution)/shard_map/ppermute | solution.py:555
  120.2 0.1 collective-permute-start.11
  120.2 4.9 %collective-permute-done.11 = f32[64,256]{1,0:T(8,128)S(1)} collective-permute-done((f32[64,256]{1,0:T(8,128)S(1)}, f32[64,256]{1,0:T(8,128)S(1)}, u32[]{:S(2)}, u32[]{:S(2)}) %collective-permute-start.11) | collective-permute-done | bytes 65568 | tf_op jit(solution)/shard_map/ppermute | solution.py:560
  125.2 0.6 collective-permute-start.12
  125.7 3.7 %collective-permute-done.12 = f32[64,256]{1,0:T(8,128)S(1)} collective-permute-done((f32[64,256]{1,0:T(8,128)S(1)}, f32[64,256]{1,0:T(8,128)S(1)}, u32[]{:S(2)}, u32[]{:S(2)}) %collective-permute-start.12) | collective-permute-done | bytes 65568 | tf_op jit(solution)/shard_map/ppermute | solution.py:561
  129.4 0.0 collective-permute-done.13.down1
  129.4 1.8 %collective-permute-start.14 = (f32[64,256]{1,0:T(8,128)S(1)}, f32[64,256]{1,0:T(8,128)S(1)}, u32[]{:S(2)}, u32[]{:S(2)}) collective-permute-start(f32[64,256]{1,0:T(8,128)S(1)} %collective-permute-done.12), channel_id=1, source_target_pairs={{0,24},{8,0},{16,8},{24,16},{32,56},{40,32},{48,40},{56,48},{64,88... | collective-permute-start | bytes 196616 | tf_op jit(solution)/shard_map/ppermute | solution.py:563
  131.2 2.5 %collective-permute-done.14 = f32[64,256]{1,0:T(8,128)S(1)} collective-permute-done((f32[64,256]{1,0:T(8,128)S(1)}, f32[64,256]{1,0:T(8,128)S(1)}, u32[]{:S(2)}, u32[]{:S(2)}) %collective-permute-start.14) | collective-permute-done | bytes 65568 | tf_op jit(solution)/shard_map/ppermute | solution.py:563
  133.7 0.0 collective-permute-done.7.right
  133.8 12.8 %all_to_all.10 = f32[8,64,256]{2,1,0:T(8,128)S(1)} all-to-all(f32[8,64,256]{2,1,0:T(8,128)S(1)} %broadcast_in_dim.2), channel_id=1, replica_groups=mesh['row'=16,'col'=8] {'col'}, dimensions={0} | all-to-all | bytes 1048576 | tf_op jit(solution)/shard_map/all_to_all | solution.py:549
  146.6 4.0 %collective-permute-done.16.down0 = f32[4,256,256]{2,1,0:T(8,128)S(1)} collective-permute-done((f32[4,256,256]{2,1,0:T(8,128)S(1)}, f32[4,256,256]{2,1,0:T(8,128)S(1)}, u32[]{:S(2)}, u32[]{:S(2)}) %collective-permute-start.16) | collective-permute-done | bytes 1048608 | tf_op jit(solution)/shard_map/ppermute | solution.py:538
  150.5 1.9 %shard_map.99 = f32[4,256,512]{2,1,0:T(8,128)} custom-call(f32[4,256,512]{2,1,0:T(8,128)S(1)} %get-tuple-element.37.base, f32[4,256,256]{2,1,0:T(8,128)S(1)} %collective-permute-done.7.right, f32[4,256,256]{2,1,0:T(8,128)S(1)} %collective-permute-done.16.down0, f32[4,256,256]{2,1,0:T(8,128)S(1)} %collective-permute-done.13.down1), custom_call_target="tpu_custom_call" | custom-call | flops 1048576 | bytes 7340032 | tf_op jit(solution)/shard_map/pallas_call | solution.py:524
  152.5 0.8 copy.12
  (27 shorter events, 0.1 us)
Async XLA Ops:
  0.6 11.1 %copy-start.12 = (f32[4,256,512]{2,1,0:T(8,128)S(1)}, f32[4,256,512]{2,1,0:T(8,128)}, u32[]{:S(2)}) copy-start(f32[4,256,512]{2,1,0:T(8,128)} %own.3) | copy-start | bytes 6291460
  2.7 20.7 %collective-permute-start.1 = (f32[2,256,256]{2,1,0:T(8,128)}, f32[2,256,256]{2,1,0:T(8,128)S(1)}, u32[]{:S(2)}, u32[]{:S(2)}) collective-permute-start(f32[2,256,256]{2,1,0:T(8,128)} %slice.23), channel_id=1, source_target_pairs={{8,0},{16,8},{24,16},{32,24},{40,32},{48,40},{56,48},{64,56},{72,6... | collective-permute-start | bytes 1572872 | tf_op jit(solution)/shard_map/ppermute | solution.py:538
  10.1 6.1 %copy-start.15 = (s32[8,2]{0,1:T(2,128)S(1)}, s32[8,2]{0,1:T(2,128)}, u32[]{:S(2)}) copy-start(s32[8,2]{0,1:T(2,128)} %param.10) | copy-start | bytes 196
  10.1 6.2 %copy-start = (f32[8,256,256]{2,1,0:T(8,128)S(1)}, f32[8,256,256]{2,1,0:T(8,128)}, u32[]{:S(2)}) copy-start(f32[8,256,256]{2,1,0:T(8,128)} %amp.1) | copy-start | bytes 6291460
  10.1 6.2 %copy-start.1 = (f32[2,256,256]{2,1,0:T(8,128)S(1)}, f32[2,256,256]{2,1,0:T(8,128)}, u32[]{:S(2)}) copy-start(f32[2,256,256]{2,1,0:T(8,128)} %probe.1) | copy-start | bytes 1572868
  10.1 6.2 %copy-start.2 = (bf16[2,256,256]{2,1,0:T(8,128)(2,1)S(1)}, bf16[2,256,256]{2,1,0:T(8,128)(2,1)}, u32[]{:S(2)}) copy-start(bf16[2,256,256]{2,1,0:T(8,128)(2,1)} %constant.23.clone.fold) | copy-start | bytes 786436
  10.1 21.4 %collective-permute-start = (f32[4,256,256]{2,1,0:T(8,128)}, f32[4,256,256]{2,1,0:T(8,128)}, u32[]{:S(2)}, u32[]{:S(2)}) collective-permute-start(f32[4,256,256]{2,1,0:T(8,128)} %slice.24), channel_id=1, source_target_pairs={{1,0},{2,1},{3,2},{4,3},{5,4},{6,5},{7,6},{9,8},{10,9},{11,10},{12... | collective-permute-start | bytes 3145736 | tf_op jit(solution)/shard_map/ppermute | solution.py:538
  12.9 18.7 %collective-permute-start.3 = (f32[2,256,256]{2,1,0:T(8,128)}, f32[2,256,256]{2,1,0:T(8,128)}, u32[]{:S(2)}, u32[]{:S(2)}) collective-permute-start(f32[2,256,256]{2,1,0:T(8,128)} %get-tuple-element.52), channel_id=1, source_target_pairs={{8,0},{16,8},{24,16},{32,24},{40,32},{48,40},{56,48},{64,56},{72,6... | collective-permute-start | bytes 1572872 | tf_op jit(solution)/shard_map/ppermute | solution.py:538
  16.2 8.5 %copy-start.14 = (f32[2,256,256]{2,1,0:T(8,128)S(1)}, f32[2,256,256]{2,1,0:T(8,128)}, u32[]{:S(2)}) copy-start(f32[2,256,256]{2,1,0:T(8,128)} %get-tuple-element.53) | copy-start | bytes 1572868
  16.2 12.0 %copy-start.13 = (f32[2,256,256]{2,1,0:T(8,128)S(1)}, f32[2,256,256]{2,1,0:T(8,128)}, u32[]{:S(2)}) copy-start(f32[2,256,256]{2,1,0:T(8,128)} %get-tuple-element.35) | copy-start | bytes 1572868
  16.3 24.9 %copy-start.3 = (s32[17]{0:T(128)}, s32[17]{0:T(128)S(1)}, u32[]{:S(2)}) copy-start(s32[17]{0:T(128)S(1)} %pad_add_fusion.meta) | copy-start | bytes 208
  20.0 2.0 %copy-start.5 = (f32[8,2,256,256]{3,2,1,0:T(8,128)}, f32[8,2,256,256]{3,2,1,0:T(8,128)S(1)}, u32[]{:S(2)}) copy-start(f32[8,2,256,256]{3,2,1,0:T(8,128)S(1)} %get-tuple-element.31.turned.turned_in) | copy-start | bytes 12582916
  22.0 1.3 copy-start.6
  23.4 17.9 %copy-start.10 = (f32[2,256,256]{2,1,0:T(8,128)}, f32[2,256,256]{2,1,0:T(8,128)S(1)}, u32[]{:S(2)}) copy-start(f32[2,256,256]{2,1,0:T(8,128)S(1)} %collective-permute-done.1.down0.down0_one) | copy-start | bytes 1572868
  23.4 8.2 %collective-permute-start.4 = (f32[2,256,256]{2,1,0:T(8,128)S(1)}, f32[2,256,256]{2,1,0:T(8,128)S(1)}, u32[]{:S(2)}, u32[]{:S(2)}) collective-permute-start(f32[2,256,256]{2,1,0:T(8,128)S(1)} %collective-permute-done.1.down0.down0_one), channel_id=1, source_target_pairs={{1,0},{2,1},{3,2},{4,3},{5,4},{6,5},{7,6},{9,8},{10,9},{11,10},{12... | collective-permute-start | bytes 1572872 | tf_op jit(solution)/shard_map/ppermute | solution.py:538
  24.7 18.0 %collective-permute-start.2 = (f32[2,256,256]{2,1,0:T(8,128)S(1)}, f32[2,256,256]{2,1,0:T(8,128)S(1)}, u32[]{:S(2)}, u32[]{:S(2)}) collective-permute-start(f32[2,256,256]{2,1,0:T(8,128)S(1)} %copy-done.14), channel_id=1, source_target_pairs={{8,0},{16,8},{24,16},{32,24},{40,32},{48,40},{56,48},{64,56},{72,6... | collective-permute-start | bytes 1572872 | tf_op jit(solution)/shard_map/ppermute | solution.py:538
  28.2 24.7 %collective-permute-start.5 = (f32[2,256,256]{2,1,0:T(8,128)S(1)}, f32[2,256,256]{2,1,0:T(8,128)S(1)}, u32[]{:S(2)}, u32[]{:S(2)}) collective-permute-start(f32[2,256,256]{2,1,0:T(8,128)S(1)} %copy-done.13), channel_id=1, source_target_pairs={{8,0},{16,8},{24,16},{32,24},{40,32},{48,40},{56,48},{64,56},{72,6... | collective-permute-start | bytes 1572872 | tf_op jit(solution)/shard_map/ppermute | solution.py:538
  31.6 9.7 %copy-start.11 = (f32[2,256,256]{2,1,0:T(8,128)}, f32[2,256,256]{2,1,0:T(8,128)S(1)}, u32[]{:S(2)}) copy-start(f32[2,256,256]{2,1,0:T(8,128)S(1)} %collective-permute-done.4.corner.corner_one) | copy-start | bytes 1572868
  42.7 10.2 %copy-start.16 = (f32[2,256,256]{2,1,0:T(8,128)}, f32[2,256,256]{2,1,0:T(8,128)S(1)}, u32[]{:S(2)}) copy-start(f32[2,256,256]{2,1,0:T(8,128)S(1)} %collective-permute-done.2.down0_two) | copy-start | bytes 1572868
  42.7 10.2 %collective-permute-start.6 = (f32[2,256,256]{2,1,0:T(8,128)S(1)}, f32[2,256,256]{2,1,0:T(8,128)S(1)}, u32[]{:S(2)}, u32[]{:S(2)}) collective-permute-start(f32[2,256,256]{2,1,0:T(8,128)S(1)} %collective-permute-done.2.down0_two), channel_id=1, source_target_pairs={{1,0},{2,1},{3,2},{4,3},{5,4},{6,5},{7,6},{9,8},{10,9},{11,10},{12... | collective-permute-start | bytes 1572872 | tf_op jit(solution)/shard_map/ppermute | solution.py:538
  52.9 0.8 copy-start.17
  52.9 1.0 copy-start.18
  53.9 29.5 %copy-start.4 = (s32[17]{0:T(128)S(1)}, s32[17]{0:T(128)}, u32[]{:S(2)}) copy-start(s32[17]{0:T(128)} %copy-done.3) | copy-start | bytes 208
  69.6 24.2 %all-to-all-start = ((f32[8,64,256]{2,1,0:T(8,128)}), f32[8,64,256]{2,1,0:T(8,128)}, u32[]{:S(2)}, u32[]{:S(2)}) async-start(f32[8,64,256]{2,1,0:T(8,128)} %bitcast.7), calls=%async_computation | async-start | bytes 1048576 | tf_op jit(solution)/shard_map/all_to_all | solution.py:544
  89.3 1.0 copy-start.7
  90.3 1.0 copy-start.8
  91.3 1.0 copy-start.9
  94.9 19.7 %collective-permute-start.15 = (f32[4,256,256]{2,1,0:T(8,128)}, f32[4,256,256]{2,1,0:T(8,128)S(1)}, u32[]{:S(2)}, u32[]{:S(2)}) collective-permute-start(f32[4,256,256]{2,1,0:T(8,128)} %copy-done.9), channel_id=1, source_target_pairs={{0,1},{1,2},{2,3},{3,4},{4,5},{5,6},{6,7},{8,9},{9,10},{10,11},{11... | collective-permute-start | bytes 3145736 | tf_op jit(solution)/shard_map/ppermute | solution.py:538
  98.8 30.6 %collective-permute-start.13 = (f32[4,256,256]{2,1,0:T(8,128)}, f32[4,256,256]{2,1,0:T(8,128)S(1)}, u32[]{:S(2)}, u32[]{:S(2)}) collective-permute-start(f32[4,256,256]{2,1,0:T(8,128)} %copy-done.8), channel_id=1, source_target_pairs={{0,8},{8,16},{16,24},{24,32},{32,40},{40,48},{48,56},{56,64},{64,7... | collective-permute-start | bytes 3145736 | tf_op jit(solution)/shard_map/ppermute | solution.py:538
  102.0 31.7 %collective-permute-start.7 = (f32[4,256,256]{2,1,0:T(8,128)}, f32[4,256,256]{2,1,0:T(8,128)S(1)}, u32[]{:S(2)}, u32[]{:S(2)}) collective-permute-start(f32[4,256,256]{2,1,0:T(8,128)} %copy-done.7), channel_id=1, source_target_pairs={{0,1},{1,2},{2,3},{3,4},{4,5},{5,6},{6,7},{8,9},{9,10},{10,11},{11... | collective-permute-start | bytes 3145736 | tf_op jit(solution)/shard_map/ppermute | solution.py:538
  103.6 5.5 %collective-permute-start.8 = (f32[64,256]{1,0:T(8,128)S(1)}, f32[64,256]{1,0:T(8,128)S(1)}, u32[]{:S(2)}, u32[]{:S(2)}) collective-permute-start(f32[64,256]{1,0:T(8,128)S(1)} %reduce_sum.9), channel_id=1, source_target_pairs={{0,96},{8,104},{16,112},{24,120},{32,0},{40,8},{48,16},{56,24},{64... | collective-permute-start | bytes 196616 | tf_op jit(solution)/shard_map/ppermute | solution.py:553
  109.2 5.5 %collective-permute-start.9 = (f32[64,256]{1,0:T(8,128)S(1)}, f32[64,256]{1,0:T(8,128)S(1)}, u32[]{:S(2)}, u32[]{:S(2)}) collective-permute-start(f32[64,256]{1,0:T(8,128)S(1)} %collective-permute-done.8), channel_id=1, source_target_pairs={{0,96},{8,104},{16,112},{24,120},{32,0},{40,8},{48,16},{56,24},{64... | collective-permute-start | bytes 196616 | tf_op jit(solution)/shard_map/ppermute | solution.py:554
  114.7 5.5 %collective-permute-start.10 = (f32[64,256]{1,0:T(8,128)S(1)}, f32[64,256]{1,0:T(8,128)S(1)}, u32[]{:S(2)}, u32[]{:S(2)}) collective-permute-start(f32[64,256]{1,0:T(8,128)S(1)} %collective-permute-done.9), channel_id=1, source_target_pairs={{0,96},{8,104},{16,112},{24,120},{32,0},{40,8},{48,16},{56,24},{64... | collective-permute-start | bytes 196616 | tf_op jit(solution)/shard_map/ppermute | solution.py:555
  114.8 35.7 %collective-permute-start.16 = (f32[4,256,256]{2,1,0:T(8,128)S(1)}, f32[4,256,256]{2,1,0:T(8,128)S(1)}, u32[]{:S(2)}, u32[]{:S(2)}) collective-permute-start(f32[4,256,256]{2,1,0:T(8,128)S(1)} %add.27), channel_id=1, source_target_pairs={{0,8},{8,16},{16,24},{24,32},{32,40},{40,48},{48,56},{56,64},{64,7... | collective-permute-start | bytes 3145736 | tf_op jit(solution)/shard_map/ppermute | solution.py:538
  120.2 5.0 %collective-permute-start.11 = (f32[64,256]{1,0:T(8,128)S(1)}, f32[64,256]{1,0:T(8,128)S(1)}, u32[]{:S(2)}, u32[]{:S(2)}) collective-permute-start(f32[64,256]{1,0:T(8,128)S(1)} %add_add_fusion.1), channel_id=1, source_target_pairs={{0,24},{8,0},{16,8},{24,16},{32,56},{40,32},{48,40},{56,48},{64,88... | collective-permute-start | bytes 196616 | tf_op jit(solution)/shard_map/ppermute | solution.py:560
  125.2 4.3 %collective-permute-start.12 = (f32[64,256]{1,0:T(8,128)S(1)}, f32[64,256]{1,0:T(8,128)S(1)}, u32[]{:S(2)}, u32[]{:S(2)}) collective-permute-start(f32[64,256]{1,0:T(8,128)S(1)} %collective-permute-done.11), channel_id=1, source_target_pairs={{0,24},{8,0},{16,8},{24,16},{32,56},{40,32},{48,40},{56,48},{64,88... | collective-permute-start | bytes 196616 | tf_op jit(solution)/shard_map/ppermute | solution.py:561
  129.4 4.3 %collective-permute-start.14 = (f32[64,256]{1,0:T(8,128)S(1)}, f32[64,256]{1,0:T(8,128)S(1)}, u32[]{:S(2)}, u32[]{:S(2)}) collective-permute-start(f32[64,256]{1,0:T(8,128)S(1)} %collective-permute-done.12), channel_id=1, source_target_pairs={{0,24},{8,0},{16,8},{24,16},{32,56},{40,32},{48,40},{56,48},{64,88... | collective-permute-start | bytes 196616 | tf_op jit(solution)/shard_map/ppermute | solution.py:563
where the time goes:
time: 154 us; the launch traced here: 153 us
  starting transfers between devices  45.2 us (29%)
  waiting for transfers between devices  41.8 us (27%)
  Pallas kernels  36.9 us (24%)
  local copies, waits for them, and re-layouts  13.6 us (9%)
  blocking collectives  12.8 us (8%)
  between operations  1.59 us (1%)
    ppermute x11, starting transfers between devices, shift(): lax.ppermute(value, axis, [(source, source + steps) for source in range(f...  28.4 us
    pallas_call x1, Pallas kernels, second_call(): call(second_kernel, SLOTS // GROUP, [SCALARS] + [ANYWHERE] * 10 + [WHOLE]...  15.7 us
    ppermute x11, waiting for transfers between devices, shift(): lax.ppermute(value, axis, [(source, source + steps) for source in range(f...  15.6 us
    all_to_all x1, starting transfers between devices, add_shares(): return lax.all_to_all(shares, axis, 0, 0, tiled=True).sum(axis=0)  13.8 us
    all_to_all x1, blocking collectives, hand_out(): return lax.all_to_all(spread, axis, 0, 0, tiled=True)  12.8 us
    pallas_call x1, Pallas kernels, first_call(): call(first_kernel, SLOTS // GROUP, [SCALARS] + [ANYWHERE] * 3 + [WHOLE, W...  9.69 us
    unnamed x39, local copies, waits for them, and re-layouts  8.08 us
    pallas_call x1, Pallas kernels, third_call(): call(third_kernel, SLOTS // ADDED, [SCALARS, pl.BlockSpec((ADDED, 4, W, W...  5.92 us
  transfers between devices with their start and end apart: 18, of which 11 were waited for; matrix products, arithmetic and copies ran while one was open for 2% of the time, Pallas kernels for 13%

commit v1 on v0

--- a/solution.py
+++ b/solution.py
@@ -508,7 +508,7 @@
         [shape(4, W, TC)] + [shape(4, W, W)] * 4,
         [pltpu.VMEM((2, 4, W, EXT), F32), pltpu.SemaphoreType.DMA((5,))],
         24,
-        40,
+        60,
     )(*args)
 
 

time: 154 us -> 155 us (level)
  local copies, waits for them, and re-layouts: 13.6 us -> 10.7 us
  starting transfers between devices: 45.2 us -> 47.9 us
  Pallas kernels: 36.9 us -> 38.7 us
    all_to_all x1, starting transfers between devices: 13.8 us -> 17.2 us  [add_shares(): return lax.all_to_all(shares, axis, 0, 0, tiled=True).sum(axis=0)]
    unnamed x39 -> x33, local copies, waits for them, and re-layouts: 8.08 us -> 5.12 us
    pallas_call x1, Pallas kernels: 5.92 us -> 7.75 us  [third_call(): call(third_kernel, SLOTS // ADDED, [SCALARS, pl.BlockSpec((ADDED, 4, W, W...]
  transfers between devices with their start and end apart: 18 -> 18, of which waited for: 11 -> 11; matrix products, arithmetic and copies ran while one was open for 2% -> 3% of each run, Pallas kernels for 13% -> 14%
where the time goes in v1:
time: 155 us; the launch traced here: 154 us
  starting transfers between devices  47.9 us (31%)
  waiting for transfers between devices  40.6 us (26%)
  Pallas kernels  38.7 us (25%)
  blocking collectives  13.4 us (9%)
  local copies, waits for them, and re-layouts  10.7 us (7%)
  between operations  1.57 us (1%)
    ppermute x11, starting transfers between devices, shift(): lax.ppermute(value, axis, [(source, source + steps) for source in range(f...  27.3 us
    all_to_all x1, starting transfers between devices, add_shares(): return lax.all_to_all(shares, axis, 0, 0, tiled=True).sum(axis=0)  17.2 us
    pallas_call x1, Pallas kernels, second_call(): call(second_kernel, SLOTS // GROUP, [SCALARS] + [ANYWHERE] * 10 + [WHOLE]...  15.7 us
    ppermute x11, waiting for transfers between devices, shift(): lax.ppermute(value, axis, [(source, source + steps) for source in range(f...  15 us
    all_to_all x1, blocking collectives, hand_out(): return lax.all_to_all(spread, axis, 0, 0, tiled=True)  13.4 us
    pallas_call x1, Pallas kernels, first_call(): call(first_kernel, SLOTS // GROUP, [SCALARS] + [ANYWHERE] * 3 + [WHOLE, W...  9.68 us
    pallas_call x1, Pallas kernels, third_call(): call(third_kernel, SLOTS // ADDED, [SCALARS, pl.BlockSpec((ADDED, 4, W, W...  7.75 us
    ppermute x1, waiting for transfers between devices, ring_sum(): second = lax.ppermute(first, 'row', pairs)  5.47 us
  transfers between devices with their start and end apart: 18, of which 11 were waited for; matrix products, arithmetic and copies ran while one was open for 3% of the time, Pallas kernels for 14%

profile of v1, /device:TPU:6, one launch (start us, length us, event | category | flops | bytes accessed | tf_op | source)
XLA Modules:
  0.0 154.3 jit_solution(17077134022857692375)
XLA Ops:
  0.6 0.0 copy-start.9
  0.6 2.0 %slice.23 = f32[2,256,256]{2,1,0:T(8,128)} slice(f32[4,256,512]{2,1,0:T(8,128)} %own.3), slice={[0:2], [0:256], [0:256]} | slice | bytes 1048576 | tf_op jit(solution)/shard_map/slice | solution.py:573
  2.7 5.2 %collective-permute-start.1 = (f32[2,256,256]{2,1,0:T(8,128)}, f32[2,256,256]{2,1,0:T(8,128)S(1)}, u32[]{:S(2)}, u32[]{:S(2)}) collective-permute-start(f32[2,256,256]{2,1,0:T(8,128)} %slice.23), channel_id=1, source_target_pairs={{8,0},{16,8},{24,16},{32,24},{40,32},{48,40},{56,48},{64,56},{72,6... | collective-permute-start | bytes 1572872 | tf_op jit(solution)/shard_map/ppermute | solution.py:538
  7.8 2.3 %slice.24 = f32[4,256,256]{2,1,0:T(8,128)} slice(f32[4,256,512]{2,1,0:T(8,128)} %own.3), slice={[0:4], [0:256], [0:256]} | slice | bytes 2097152 | tf_op jit(solution)/shard_map/slice | solution.py:576
  10.2 1.6 %collective-permute-start = (f32[4,256,256]{2,1,0:T(8,128)}, f32[4,256,256]{2,1,0:T(8,128)}, u32[]{:S(2)}, u32[]{:S(2)}) collective-permute-start(f32[4,256,256]{2,1,0:T(8,128)} %slice.24), channel_id=1, source_target_pairs={{1,0},{2,1},{3,2},{4,3},{5,4},{6,5},{7,6},{9,8},{10,9},{11,10},{12... | collective-permute-start | bytes 3145736 | tf_op jit(solution)/shard_map/ppermute | solution.py:538
  11.7 0.0 copy-done.9
  11.7 1.2 fusion
  12.9 2.6 %collective-permute-start.3 = (f32[2,256,256]{2,1,0:T(8,128)}, f32[2,256,256]{2,1,0:T(8,128)}, u32[]{:S(2)}, u32[]{:S(2)}) collective-permute-start(f32[2,256,256]{2,1,0:T(8,128)} %get-tuple-element.52), channel_id=1, source_target_pairs={{8,0},{16,8},{24,16},{32,24},{40,32},{48,40},{56,48},{64,56},{72,6... | collective-permute-start | bytes 1572872 | tf_op jit(solution)/shard_map/ppermute | solution.py:538
  16.2 0.0 copy-done.12
  16.2 0.0 copy-start.11
  16.2 0.0 copy-start.10
  16.2 0.1 pad_add_fusion.meta
  16.3 0.0 copy-done.1
  16.3 0.0 copy-done.2
  16.3 0.0 copy-done.3
  16.3 3.7 %shard_map.95 = (f32[8,256,256]{2,1,0:T(8,128)S(1)}, f32[8,2,256,256]{3,2,1,0:T(8,128)S(1)}) custom-call(s32[17]{0:T(128)S(1)} %pad_add_fusion.meta, f32[2,256,256]{2,1,0:T(8,128)S(1)} %copy-done.2, f32[8,256,256]{2,1,0:T(8,128)S(1)} %copy-done.1, bf16[2,256,256]{2,1,0:T(8,128)(2,1)S(1)} %copy-done.3), custom_call_target="tpu_custom_call" | custom-call | tf_op jit(solution)/shard_map/pallas_call | solution.py:449
  20.0 2.0 %copy-done.5 = f32[8,2,256,256]{3,2,1,0:T(8,128)} copy-done((f32[8,2,256,256]{3,2,1,0:T(8,128)}, f32[8,2,256,256]{3,2,1,0:T(8,128)S(1)}, u32[]{:S(2)}) %copy-start.5) | copy-done | bytes 4194328
  22.0 1.3 copy-done.6
  23.3 0.0 collective-permute-done.1.down0.down0_one
  23.3 1.3 collective-permute-start.4
  24.6 3.5 %collective-permute-start.2 = (f32[2,256,256]{2,1,0:T(8,128)S(1)}, f32[2,256,256]{2,1,0:T(8,128)S(1)}, u32[]{:S(2)}, u32[]{:S(2)}) collective-permute-start(f32[2,256,256]{2,1,0:T(8,128)S(1)} %copy-done.11), channel_id=1, source_target_pairs={{8,0},{16,8},{24,16},{32,24},{40,32},{48,40},{56,48},{64,56},{72,6... | collective-permute-start | bytes 1572872 | tf_op jit(solution)/shard_map/ppermute | solution.py:538
  28.2 1.9 %collective-permute-start.5 = (f32[2,256,256]{2,1,0:T(8,128)S(1)}, f32[2,256,256]{2,1,0:T(8,128)S(1)}, u32[]{:S(2)}, u32[]{:S(2)}) collective-permute-start(f32[2,256,256]{2,1,0:T(8,128)S(1)} %copy-done.10), channel_id=1, source_target_pairs={{8,0},{16,8},{24,16},{32,24},{40,32},{48,40},{56,48},{64,56},{72,6... | collective-permute-start | bytes 1572872 | tf_op jit(solution)/shard_map/ppermute | solution.py:538
  30.1 1.4 collective-permute-done.3.down1.down1_one
  31.6 0.0 collective-permute-done.right
  31.6 0.0 collective-permute-done.4.corner.corner_one
  31.6 9.7 %shard_map.96.prop_in = f32[8,2,256,256]{3,2,1,0:T(8,128)} custom-call(s32[17]{0:T(128)S(1)} %pad_add_fusion.meta, f32[4,256,512]{2,1,0:T(8,128)} %own.3, f32[4,256,256]{2,1,0:T(8,128)} %collective-permute-done.right, f32[2,256,256]{2,1,0:T(8,128)S(1)} %collective-permute-done.1.down0.down0_one, f32[2,256,256]{2,1,0:T(8,128)} %collective-permute-done.3.down1.down1_one, ...), custom_call_target="tpu_custom_call" | custom-call | flops 6442450944 | bytes 6291456 | tf_op jit(solution)/shard_map/pallas_call | solution.py:465
  41.2 0.0 copy-done.4
  41.3 0.0 copy-done.7
  41.3 0.0 copy-done.8
  41.3 1.4 collective-permute-done.2.down0_two
  42.7 1.5 collective-permute-start.6
  44.2 8.8 %collective-permute-done.5.down1_two = f32[2,256,256]{2,1,0:T(8,128)S(1)} collective-permute-done((f32[2,256,256]{2,1,0:T(8,128)S(1)}, f32[2,256,256]{2,1,0:T(8,128)S(1)}, u32[]{:S(2)}, u32[]{:S(2)}) %collective-permute-start.5) | collective-permute-done | bytes 524320 | tf_op jit(solution)/shard_map/ppermute | solution.py:538
  52.9 0.0 collective-permute-done.6.corner_two
  52.9 0.8 copy-done.14
  53.7 0.2 copy-done.15
  53.9 15.7 %shard_map.97 = (f32[2,256,256]{2,1,0:T(8,128)}, f32[8,4,256,256]{3,2,1,0:T(8,128)}) custom-call(s32[17]{0:T(128)} %copy-done.4, f32[4,256,512]{2,1,0:T(8,128)} %own.3, f32[4,256,256]{2,1,0:T(8,128)} %collective-permute-done.right, f32[2,256,256]{2,1,0:T(8,128)} %copy-done.7, f32[2,256,256]{2,1,0:T(8,128)} %copy-done.13, ...), custom_call_target="tpu_custom_call" | custom-call | flops 12884901888 | bytes 12582912 | tf_op jit(solution)/shard_map/pallas_call | solution.py:482
  69.6 17.2 %all-to-all-start = ((f32[8,64,256]{2,1,0:T(8,128)}), f32[8,64,256]{2,1,0:T(8,128)S(1)}, u32[]{:S(2)}, u32[]{:S(2)}) async-start(f32[8,64,256]{2,1,0:T(8,128)} %bitcast.7), calls=%async_computation | async-start | bytes 1048576 | tf_op jit(solution)/shard_map/all_to_all | solution.py:544
  86.8 7.8 %shard_map.98 = (f32[4,256,512]{2,1,0:T(8,128)}, f32[4,256,256]{2,1,0:T(8,128)}, f32[4,256,256]{2,1,0:T(8,128)}, f32[4,256,256]{2,1,0:T(8,128)}, f32[4,256,256]{2,1,0:T(8,128)}) custom-call(s32[17]{0:T(128)} %copy-done.4, f32[8,4,256,256]{3,2,1,0:T(8,128)} %get-tuple-element.36.grads), custom_call_target="tpu_custom_call" | custom-call | flops 6442450944 | bytes 6291456 | tf_op jit(solution)/shard_map/pallas_call | solution.py:503
  94.5 2.6 %all-to-all-done = f32[8,64,256]{2,1,0:T(8,128)S(1)} async-done(((f32[8,64,256]{2,1,0:T(8,128)}), f32[8,64,256]{2,1,0:T(8,128)S(1)}, u32[]{:S(2)}, u32[]{:S(2)}) %all-to-all-start) | async-done | bytes 524320 | tf_op jit(solution)/shard_map/all_to_all | solution.py:544
  97.1 0.0 copy-start
  97.2 1.7 %collective-permute-start.15 = (f32[4,256,256]{2,1,0:T(8,128)}, f32[4,256,256]{2,1,0:T(8,128)S(1)}, u32[]{:S(2)}, u32[]{:S(2)}) collective-permute-start(f32[4,256,256]{2,1,0:T(8,128)} %get-tuple-element.49), channel_id=1, source_target_pairs={{0,1},{1,2},{2,3},{3,4},{4,5},{5,6},{6,7},{8,9},{9,10},{10,11},{11... | collective-permute-start | bytes 3145736 | tf_op jit(solution)/shard_map/ppermute | solution.py:538
  98.9 3.2 %collective-permute-start.13 = (f32[4,256,256]{2,1,0:T(8,128)}, f32[4,256,256]{2,1,0:T(8,128)S(1)}, u32[]{:S(2)}, u32[]{:S(2)}) collective-permute-start(f32[4,256,256]{2,1,0:T(8,128)} %get-tuple-element.45), channel_id=1, source_target_pairs={{0,8},{8,16},{16,24},{24,32},{32,40},{40,48},{48,56},{56,64},{64,7... | collective-permute-start | bytes 3145736 | tf_op jit(solution)/shard_map/ppermute | solution.py:538
  102.1 2.7 %collective-permute-start.7 = (f32[4,256,256]{2,1,0:T(8,128)}, f32[4,256,256]{2,1,0:T(8,128)S(1)}, u32[]{:S(2)}, u32[]{:S(2)}) collective-permute-start(f32[4,256,256]{2,1,0:T(8,128)} %get-tuple-element.43), channel_id=1, source_target_pairs={{0,1},{1,2},{2,3},{3,4},{4,5},{5,6},{6,7},{8,9},{9,10},{10,11},{11... | collective-permute-start | bytes 3145736 | tf_op jit(solution)/shard_map/ppermute | solution.py:538
  104.8 0.6 collective-permute-start.8
  105.4 4.9 %collective-permute-done.8 = f32[64,256]{1,0:T(8,128)S(1)} collective-permute-done((f32[64,256]{1,0:T(8,128)S(1)}, f32[64,256]{1,0:T(8,128)S(1)}, u32[]{:S(2)}, u32[]{:S(2)}) %collective-permute-start.8) | collective-permute-done | bytes 65568 | tf_op jit(solution)/shard_map/ppermute | solution.py:553
  110.3 0.0 collective-permute-start.9
  110.3 5.5 %collective-permute-done.9 = f32[64,256]{1,0:T(8,128)S(1)} collective-permute-done((f32[64,256]{1,0:T(8,128)S(1)}, f32[64,256]{1,0:T(8,128)S(1)}, u32[]{:S(2)}, u32[]{:S(2)}) %collective-permute-start.9) | collective-permute-done | bytes 65568 | tf_op jit(solution)/shard_map/ppermute | solution.py:554
  115.8 0.0 collective-permute-start.10
  115.8 0.0 collective-permute-done.15
  115.8 1.4 add.27
  117.2 2.2 %collective-permute-start.16 = (f32[4,256,256]{2,1,0:T(8,128)S(1)}, f32[4,256,256]{2,1,0:T(8,128)S(1)}, u32[]{:S(2)}, u32[]{:S(2)}) collective-permute-start(f32[4,256,256]{2,1,0:T(8,128)S(1)} %add.27), channel_id=1, source_target_pairs={{0,8},{8,16},{16,24},{24,32},{32,40},{40,48},{48,56},{56,64},{64,7... | collective-permute-start | bytes 3145736 | tf_op jit(solution)/shard_map/ppermute | solution.py:538
  119.4 1.9 %collective-permute-done.10 = f32[64,256]{1,0:T(8,128)S(1)} collective-permute-done((f32[64,256]{1,0:T(8,128)S(1)}, f32[64,256]{1,0:T(8,128)S(1)}, u32[]{:S(2)}, u32[]{:S(2)}) %collective-permute-start.10) | collective-permute-done | bytes 65568 | tf_op jit(solution)/shard_map/ppermute | solution.py:555
  121.3 0.2 collective-permute-start.11
  121.4 4.8 %collective-permute-done.11 = f32[64,256]{1,0:T(8,128)S(1)} collective-permute-done((f32[64,256]{1,0:T(8,128)S(1)}, f32[64,256]{1,0:T(8,128)S(1)}, u32[]{:S(2)}, u32[]{:S(2)}) %collective-permute-start.11) | collective-permute-done | bytes 65568 | tf_op jit(solution)/shard_map/ppermute | solution.py:560
  126.2 0.7 collective-permute-start.12
  126.9 3.6 %collective-permute-done.12 = f32[64,256]{1,0:T(8,128)S(1)} collective-permute-done((f32[64,256]{1,0:T(8,128)S(1)}, f32[64,256]{1,0:T(8,128)S(1)}, u32[]{:S(2)}, u32[]{:S(2)}) %collective-permute-start.12) | collective-permute-done | bytes 65568 | tf_op jit(solution)/shard_map/ppermute | solution.py:561
  130.5 0.0 collective-permute-done.13.down1
  130.5 1.9 %collective-permute-start.14 = (f32[64,256]{1,0:T(8,128)S(1)}, f32[64,256]{1,0:T(8,128)S(1)}, u32[]{:S(2)}, u32[]{:S(2)}) collective-permute-start(f32[64,256]{1,0:T(8,128)S(1)} %collective-permute-done.12), channel_id=1, source_target_pairs={{0,24},{8,0},{16,8},{24,16},{32,56},{40,32},{48,40},{56,48},{64,88... | collective-permute-start | bytes 196616 | tf_op jit(solution)/shard_map/ppermute | solution.py:563
  132.4 2.3 %collective-permute-done.14 = f32[64,256]{1,0:T(8,128)S(1)} collective-permute-done((f32[64,256]{1,0:T(8,128)S(1)}, f32[64,256]{1,0:T(8,128)S(1)}, u32[]{:S(2)}, u32[]{:S(2)}) %collective-permute-start.14) | collective-permute-done | bytes 65568 | tf_op jit(solution)/shard_map/ppermute | solution.py:563
  134.8 0.0 collective-permute-done.7.right
  134.8 13.4 %all_to_all.10 = f32[8,64,256]{2,1,0:T(8,128)S(1)} all-to-all(f32[8,64,256]{2,1,0:T(8,128)S(1)} %broadcast_in_dim.2), channel_id=1, replica_groups=mesh['row'=16,'col'=8] {'col'}, dimensions={0} | all-to-all | bytes 1048576 | tf_op jit(solution)/shard_map/all_to_all | solution.py:549
  148.2 3.4 %collective-permute-done.16.down0 = f32[4,256,256]{2,1,0:T(8,128)S(1)} collective-permute-done((f32[4,256,256]{2,1,0:T(8,128)S(1)}, f32[4,256,256]{2,1,0:T(8,128)S(1)}, u32[]{:S(2)}, u32[]{:S(2)}) %collective-permute-start.16) | collective-permute-done | bytes 1048608 | tf_op jit(solution)/shard_map/ppermute | solution.py:538
  151.6 1.9 %shard_map.99 = f32[4,256,512]{2,1,0:T(8,128)} custom-call(f32[4,256,512]{2,1,0:T(8,128)S(1)} %copy-done, f32[4,256,256]{2,1,0:T(8,128)S(1)} %collective-permute-done.7.right, f32[4,256,256]{2,1,0:T(8,128)S(1)} %collective-permute-done.16.down0, f32[4,256,256]{2,1,0:T(8,128)S(1)} %collective-permute-done.13.down1), custom_call_target="tpu_custom_call" | custom-call | flops 1048576 | bytes 7340032 | tf_op jit(solution)/shard_map/pallas_call | solution.py:524
  153.5 0.8 copy.12
  (21 shorter events, 0.1 us)
Async XLA Ops:
  0.6 11.1 %copy-start.9 = (f32[4,256,512]{2,1,0:T(8,128)S(1)}, f32[4,256,512]{2,1,0:T(8,128)}, u32[]{:S(2)}) copy-start(f32[4,256,512]{2,1,0:T(8,128)} %own.3) | copy-start | bytes 6291460
  2.7 20.7 %collective-permute-start.1 = (f32[2,256,256]{2,1,0:T(8,128)}, f32[2,256,256]{2,1,0:T(8,128)S(1)}, u32[]{:S(2)}, u32[]{:S(2)}) collective-permute-start(f32[2,256,256]{2,1,0:T(8,128)} %slice.23), channel_id=1, source_target_pairs={{8,0},{16,8},{24,16},{32,24},{40,32},{48,40},{56,48},{64,56},{72,6... | collective-permute-start | bytes 1572872 | tf_op jit(solution)/shard_map/ppermute | solution.py:538
  10.1 6.1 %copy-start.12 = (s32[8,2]{0,1:T(2,128)S(1)}, s32[8,2]{0,1:T(2,128)}, u32[]{:S(2)}) copy-start(s32[8,2]{0,1:T(2,128)} %param.10) | copy-start | bytes 196
  10.1 6.2 %copy-start.1 = (f32[8,256,256]{2,1,0:T(8,128)S(1)}, f32[8,256,256]{2,1,0:T(8,128)}, u32[]{:S(2)}) copy-start(f32[8,256,256]{2,1,0:T(8,128)} %amp.1) | copy-start | bytes 6291460
  10.1 6.2 %copy-start.2 = (f32[2,256,256]{2,1,0:T(8,128)S(1)}, f32[2,256,256]{2,1,0:T(8,128)}, u32[]{:S(2)}) copy-start(f32[2,256,256]{2,1,0:T(8,128)} %probe.1) | copy-start | bytes 1572868
  10.1 6.2 %copy-start.3 = (bf16[2,256,256]{2,1,0:T(8,128)(2,1)S(1)}, bf16[2,256,256]{2,1,0:T(8,128)(2,1)}, u32[]{:S(2)}) copy-start(bf16[2,256,256]{2,1,0:T(8,128)(2,1)} %constant.23.clone.fold) | copy-start | bytes 786436
  10.2 21.4 %collective-permute-start = (f32[4,256,256]{2,1,0:T(8,128)}, f32[4,256,256]{2,1,0:T(8,128)}, u32[]{:S(2)}, u32[]{:S(2)}) collective-permute-start(f32[4,256,256]{2,1,0:T(8,128)} %slice.24), channel_id=1, source_target_pairs={{1,0},{2,1},{3,2},{4,3},{5,4},{6,5},{7,6},{9,8},{10,9},{11,10},{12... | collective-permute-start | bytes 3145736 | tf_op jit(solution)/shard_map/ppermute | solution.py:538
  12.9 18.6 %collective-permute-start.3 = (f32[2,256,256]{2,1,0:T(8,128)}, f32[2,256,256]{2,1,0:T(8,128)}, u32[]{:S(2)}, u32[]{:S(2)}) collective-permute-start(f32[2,256,256]{2,1,0:T(8,128)} %get-tuple-element.52), channel_id=1, source_target_pairs={{8,0},{16,8},{24,16},{32,24},{40,32},{48,40},{56,48},{64,56},{72,6... | collective-permute-start | bytes 1572872 | tf_op jit(solution)/shard_map/ppermute | solution.py:538
  16.2 8.4 %copy-start.11 = (f32[2,256,256]{2,1,0:T(8,128)S(1)}, f32[2,256,256]{2,1,0:T(8,128)}, u32[]{:S(2)}) copy-start(f32[2,256,256]{2,1,0:T(8,128)} %get-tuple-element.53) | copy-start | bytes 1572868
  16.2 11.9 %copy-start.10 = (f32[2,256,256]{2,1,0:T(8,128)S(1)}, f32[2,256,256]{2,1,0:T(8,128)}, u32[]{:S(2)}) copy-start(f32[2,256,256]{2,1,0:T(8,128)} %get-tuple-element.35) | copy-start | bytes 1572868
  16.3 24.9 %copy-start.4 = (s32[17]{0:T(128)}, s32[17]{0:T(128)S(1)}, u32[]{:S(2)}) copy-start(s32[17]{0:T(128)S(1)} %pad_add_fusion.meta) | copy-start | bytes 208
  20.0 2.0 %copy-start.5 = (f32[8,2,256,256]{3,2,1,0:T(8,128)}, f32[8,2,256,256]{3,2,1,0:T(8,128)S(1)}, u32[]{:S(2)}) copy-start(f32[8,2,256,256]{3,2,1,0:T(8,128)S(1)} %get-tuple-element.31.turned.turned_in) | copy-start | bytes 12582916
  22.0 1.3 copy-start.6
  23.3 17.9 %copy-start.7 = (f32[2,256,256]{2,1,0:T(8,128)}, f32[2,256,256]{2,1,0:T(8,128)S(1)}, u32[]{:S(2)}) copy-start(f32[2,256,256]{2,1,0:T(8,128)S(1)} %collective-permute-done.1.down0.down0_one) | copy-start | bytes 1572868
  23.3 8.2 %collective-permute-start.4 = (f32[2,256,256]{2,1,0:T(8,128)S(1)}, f32[2,256,256]{2,1,0:T(8,128)S(1)}, u32[]{:S(2)}, u32[]{:S(2)}) collective-permute-start(f32[2,256,256]{2,1,0:T(8,128)S(1)} %collective-permute-done.1.down0.down0_one), channel_id=1, source_target_pairs={{1,0},{2,1},{3,2},{4,3},{5,4},{6,5},{7,6},{9,8},{10,9},{11,10},{12... | collective-permute-start | bytes 1572872 | tf_op jit(solution)/shard_map/ppermute | solution.py:538
  24.6 18.0 %collective-permute-start.2 = (f32[2,256,256]{2,1,0:T(8,128)S(1)}, f32[2,256,256]{2,1,0:T(8,128)S(1)}, u32[]{:S(2)}, u32[]{:S(2)}) collective-permute-start(f32[2,256,256]{2,1,0:T(8,128)S(1)} %copy-done.11), channel_id=1, source_target_pairs={{8,0},{16,8},{24,16},{32,24},{40,32},{48,40},{56,48},{64,56},{72,6... | collective-permute-start | bytes 1572872 | tf_op jit(solution)/shard_map/ppermute | solution.py:538
  28.2 24.7 %collective-permute-start.5 = (f32[2,256,256]{2,1,0:T(8,128)S(1)}, f32[2,256,256]{2,1,0:T(8,128)S(1)}, u32[]{:S(2)}, u32[]{:S(2)}) collective-permute-start(f32[2,256,256]{2,1,0:T(8,128)S(1)} %copy-done.10), channel_id=1, source_target_pairs={{8,0},{16,8},{24,16},{32,24},{40,32},{48,40},{56,48},{64,56},{72,6... | collective-permute-start | bytes 1572872 | tf_op jit(solution)/shard_map/ppermute | solution.py:538
  31.6 9.7 %copy-start.8 = (f32[2,256,256]{2,1,0:T(8,128)}, f32[2,256,256]{2,1,0:T(8,128)S(1)}, u32[]{:S(2)}) copy-start(f32[2,256,256]{2,1,0:T(8,128)S(1)} %collective-permute-done.4.corner.corner_one) | copy-start | bytes 1572868
  42.7 10.2 %copy-start.13 = (f32[2,256,256]{2,1,0:T(8,128)}, f32[2,256,256]{2,1,0:T(8,128)S(1)}, u32[]{:S(2)}) copy-start(f32[2,256,256]{2,1,0:T(8,128)S(1)} %collective-permute-done.2.down0_two) | copy-start | bytes 1572868
  42.7 10.2 %collective-permute-start.6 = (f32[2,256,256]{2,1,0:T(8,128)S(1)}, f32[2,256,256]{2,1,0:T(8,128)S(1)}, u32[]{:S(2)}, u32[]{:S(2)}) collective-permute-start(f32[2,256,256]{2,1,0:T(8,128)S(1)} %collective-permute-done.2.down0_two), channel_id=1, source_target_pairs={{1,0},{2,1},{3,2},{4,3},{5,4},{6,5},{7,6},{9,8},{10,9},{11,10},{12... | collective-permute-start | bytes 1572872 | tf_op jit(solution)/shard_map/ppermute | solution.py:538
  52.9 0.8 copy-start.14
  52.9 1.0 copy-start.15
  69.6 27.5 %all-to-all-start = ((f32[8,64,256]{2,1,0:T(8,128)}), f32[8,64,256]{2,1,0:T(8,128)S(1)}, u32[]{:S(2)}, u32[]{:S(2)}) async-start(f32[8,64,256]{2,1,0:T(8,128)} %bitcast.7), calls=%async_computation | async-start | bytes 1048576 | tf_op jit(solution)/shard_map/all_to_all | solution.py:544
  97.1 54.5 %copy-start = (f32[4,256,512]{2,1,0:T(8,128)S(1)}, f32[4,256,512]{2,1,0:T(8,128)}, u32[]{:S(2)}) copy-start(f32[4,256,512]{2,1,0:T(8,128)} %get-tuple-element.37.base) | copy-start | bytes 6291460
  97.2 18.6 %collective-permute-start.15 = (f32[4,256,256]{2,1,0:T(8,128)}, f32[4,256,256]{2,1,0:T(8,128)S(1)}, u32[]{:S(2)}, u32[]{:S(2)}) collective-permute-start(f32[4,256,256]{2,1,0:T(8,128)} %get-tuple-element.49), channel_id=1, source_target_pairs={{0,1},{1,2},{2,3},{3,4},{4,5},{5,6},{6,7},{8,9},{9,10},{10,11},{11... | collective-permute-start | bytes 3145736 | tf_op jit(solution)/shard_map/ppermute | solution.py:538
  98.9 31.6 %collective-permute-start.13 = (f32[4,256,256]{2,1,0:T(8,128)}, f32[4,256,256]{2,1,0:T(8,128)S(1)}, u32[]{:S(2)}, u32[]{:S(2)}) collective-permute-start(f32[4,256,256]{2,1,0:T(8,128)} %get-tuple-element.45), channel_id=1, source_target_pairs={{0,8},{8,16},{16,24},{24,32},{32,40},{40,48},{48,56},{56,64},{64,7... | collective-permute-start | bytes 3145736 | tf_op jit(solution)/shard_map/ppermute | solution.py:538
  102.1 32.7 %collective-permute-start.7 = (f32[4,256,256]{2,1,0:T(8,128)}, f32[4,256,256]{2,1,0:T(8,128)S(1)}, u32[]{:S(2)}, u32[]{:S(2)}) collective-permute-start(f32[4,256,256]{2,1,0:T(8,128)} %get-tuple-element.43), channel_id=1, source_target_pairs={{0,1},{1,2},{2,3},{3,4},{4,5},{5,6},{6,7},{8,9},{9,10},{10,11},{11... | collective-permute-start | bytes 3145736 | tf_op jit(solution)/shard_map/ppermute | solution.py:538
  104.8 5.5 %collective-permute-start.8 = (f32[64,256]{1,0:T(8,128)S(1)}, f32[64,256]{1,0:T(8,128)S(1)}, u32[]{:S(2)}, u32[]{:S(2)}) collective-permute-start(f32[64,256]{1,0:T(8,128)S(1)} %reduce_sum.9), channel_id=1, source_target_pairs={{0,96},{8,104},{16,112},{24,120},{32,0},{40,8},{48,16},{56,24},{64... | collective-permute-start | bytes 196616 | tf_op jit(solution)/shard_map/ppermute | solution.py:553
  110.3 5.5 %collective-permute-start.9 = (f32[64,256]{1,0:T(8,128)S(1)}, f32[64,256]{1,0:T(8,128)S(1)}, u32[]{:S(2)}, u32[]{:S(2)}) collective-permute-start(f32[64,256]{1,0:T(8,128)S(1)} %collective-permute-done.8), channel_id=1, source_target_pairs={{0,96},{8,104},{16,112},{24,120},{32,0},{40,8},{48,16},{56,24},{64... | collective-permute-start | bytes 196616 | tf_op jit(solution)/shard_map/ppermute | solution.py:554
  115.8 5.5 %collective-permute-start.10 = (f32[64,256]{1,0:T(8,128)S(1)}, f32[64,256]{1,0:T(8,128)S(1)}, u32[]{:S(2)}, u32[]{:S(2)}) collective-permute-start(f32[64,256]{1,0:T(8,128)S(1)} %collective-permute-done.9), channel_id=1, source_target_pairs={{0,96},{8,104},{16,112},{24,120},{32,0},{40,8},{48,16},{56,24},{64... | collective-permute-start | bytes 196616 | tf_op jit(solution)/shard_map/ppermute | solution.py:555
  117.2 34.5 %collective-permute-start.16 = (f32[4,256,256]{2,1,0:T(8,128)S(1)}, f32[4,256,256]{2,1,0:T(8,128)S(1)}, u32[]{:S(2)}, u32[]{:S(2)}) collective-permute-start(f32[4,256,256]{2,1,0:T(8,128)S(1)} %add.27), channel_id=1, source_target_pairs={{0,8},{8,16},{16,24},{24,32},{32,40},{40,48},{48,56},{56,64},{64,7... | collective-permute-start | bytes 3145736 | tf_op jit(solution)/shard_map/ppermute | solution.py:538
  121.3 4.9 %collective-permute-start.11 = (f32[64,256]{1,0:T(8,128)S(1)}, f32[64,256]{1,0:T(8,128)S(1)}, u32[]{:S(2)}, u32[]{:S(2)}) collective-permute-start(f32[64,256]{1,0:T(8,128)S(1)} %add_add_fusion.1), channel_id=1, source_target_pairs={{0,24},{8,0},{16,8},{24,16},{32,56},{40,32},{48,40},{56,48},{64,88... | collective-permute-start | bytes 196616 | tf_op jit(solution)/shard_map/ppermute | solution.py:560
  126.2 4.3 %collective-permute-start.12 = (f32[64,256]{1,0:T(8,128)S(1)}, f32[64,256]{1,0:T(8,128)S(1)}, u32[]{:S(2)}, u32[]{:S(2)}) collective-permute-start(f32[64,256]{1,0:T(8,128)S(1)} %collective-permute-done.11), channel_id=1, source_target_pairs={{0,24},{8,0},{16,8},{24,16},{32,56},{40,32},{48,40},{56,48},{64,88... | collective-permute-start | bytes 196616 | tf_op jit(solution)/shard_map/ppermute | solution.py:561
  130.5 4.3 %collective-permute-start.14 = (f32[64,256]{1,0:T(8,128)S(1)}, f32[64,256]{1,0:T(8,128)S(1)}, u32[]{:S(2)}, u32[]{:S(2)}) collective-permute-start(f32[64,256]{1,0:T(8,128)S(1)} %collective-permute-done.12), channel_id=1, source_target_pairs={{0,24},{8,0},{16,8},{24,16},{32,56},{40,32},{48,40},{56,48},{64,88... | collective-permute-start | bytes 196616 | tf_op jit(solution)/shard_map/ppermute | solution.py:563

commit v2 on v0

--- a/solution.py
+++ b/solution.py
@@ -1,3 +1,4 @@
+import functools
 import math
 
 import jax
@@ -294,27 +295,25 @@
         turn_probe(meta, step * PREPARED + u, twice, turned, u)
 
 
-def first_kernel(meta, own, right, down0, down1, corner, turned, tab, prop, ext, win, sems):
-    step = pl.program_id(0)
-
-    @pl.when(step == 0)
-    def begin():
-        one = pl.ds(0, 2)
+def first_kernel(start, meta, own, right, down0, down1, corner, turned_in, hop_in, prop, ext, turned, hop, win, sems):
+    @pl.when(start < meta[0])
+    def work():
+        one, group = pl.ds(0, 2), pl.ds(start, GROUP)
         refs = (own.at[one], right.at[one], down0, down1, corner)
-        wait_copies(start_copies(tile_copies(refs, ext, sems)))
-
-    @pl.when(step * GROUP < meta[0])
-    def work():
+        started = start_copies(tile_copies(refs, ext, sems))
+        rest = start_copies([(turned_in.at[group], turned, sems.at[5]), (hop_in, hop, sems.at[6])])
+        wait_copies(started)
         for u in range(GROUP):
-            load_window(meta, step * GROUP + u, ext, (0, 1), win, u)
+            load_window(meta, start + u, ext, (0, 1), win, u)
+        wait_copies(rest)
         fields = [times(pair(turned, u), pair(win, u)) for u in range(GROUP)]
-        fields = [hop_right(f, tab, 0, False) for f in fields]
-        fields = [hop_left(f, tab, 1, False) for f in fields]
+        fields = [hop_right(f, hop, 0, False) for f in fields]
+        fields = [hop_left(f, hop, 1, False) for f in fields]
         for u, f in enumerate(fields):
             put(f, prop, u)
 
 
-def second_kernel(meta, own, right, down0_one, down0_two, down1_one, corner_one, turned_in, hop_in, prop_in, amp_in,
+def second_kernel(meta, own, right, down0_one, down0_two, down1_one, corner_one, turned_in, hop_in, prop_now, prop_later, amp_in,
                   down1_two, corner_two, dft, gprobe, win,
                   ext, acc, turned, hop, prop, amp, sems):
     step = pl.program_id(0)
@@ -326,12 +325,12 @@
     copies_two = tile_copies(refs_two, ext.at[:, two], sems.at[1])
     now, later = pl.ds(0, GROUP), pl.ds(GROUP, SLOTS - GROUP)
     copies_now = copies_two + [
-        (prop_in.at[now], prop.at[now], sems.at[2, 0]),
+        (prop_now, prop.at[now], sems.at[2, 0]),
         (amp_in.at[now], amp.at[now], sems.at[2, 1]),
     ]
     copies_later = [(hop_in, hop, sems.at[2, 2])] + copies_one + [
         (turned_in, turned, sems.at[2, 3]),
-        (prop_in.at[later], prop.at[later], sems.at[2, 4]),
+        (prop_later, prop.at[later], sems.at[2, 4]),
         (amp_in.at[later], amp.at[later], sems.at[2, 5]),
     ]
 
@@ -461,19 +460,21 @@
     )(*args)
 
 
-def first_call(*args):
+def first_call(start, products, *args):
     return call(
-        first_kernel,
-        SLOTS // GROUP,
-        [SCALARS] + [ANYWHERE] * 3 + [WHOLE, WHOLE, FIELDS, WHOLE],
-        FIELDS,
-        FIELDS_SHAPE,
+        functools.partial(first_kernel, start),
+        1,
+        [SCALARS] + [ANYWHERE] * 3 + [WHOLE, WHOLE] + [ANYWHERE] * 2,
+        pl.BlockSpec((GROUP, 2, W, W), lambda i: (0, 0, 0, 0)),
+        shape(GROUP, 2, W, W),
         [
             pltpu.VMEM((2, 2, W, EXT), F32),
             pltpu.VMEM((GROUP, 2, W, W), F32),
-            pltpu.SemaphoreType.DMA((5,)),
+            pltpu.VMEM((12, W, W), BF16),
+            pltpu.VMEM((GROUP, 2, W, W), F32),
+            pltpu.SemaphoreType.DMA((7,)),
         ],
-        24,
+        products,
         52,
     )(*args)
 
@@ -482,7 +483,7 @@
     return call(
         second_kernel,
         SLOTS // GROUP,
-        [SCALARS] + [ANYWHERE] * 10 + [WHOLE] * 3,
+        [SCALARS] + [ANYWHERE] * 11 + [WHOLE] * 3,
         [WHOLE, pl.BlockSpec((GROUP, 4, W, W), lambda i: (i, 0, 0, 0))],
         [shape(2, W, W), shape(SLOTS, 4, W, W)],
         [
@@ -579,11 +580,13 @@
     down0_one, turned, last_part = lax.optimization_barrier((down0_one, turned, rest[2:, :, W:]))
     corner_one = shift(down0_one, "col", -1)
     down1_two = shift(last_part, "row", -1)
-    prop = first_call(meta, object_slab, right, down0_one, down1_one, corner_one, turned, hop)
-    down0_two, prop = lax.optimization_barrier((down0_two, prop))
+    near = (meta, object_slab, right, down0_one, down1_one, corner_one, turned, hop)
+    prop_now = first_call(0, 12, *near)
+    down0_two, prop_now, near = lax.optimization_barrier((down0_two, prop_now, near))
     corner_two = shift(down0_two, "col", -1)
+    prop_later = first_call(GROUP, 0, *near)
     gprobe, grads = second_call(
-        meta, object_slab, right, down0_one, down0_two, down1_one, corner_one, turned, hop, prop, amp,
+        meta, object_slab, right, down0_one, down0_two, down1_one, corner_one, turned, hop, prop_now, prop_later, amp,
         down1_two, corner_two, dft,
     )
     share = add_shares(gprobe, "col")

time: 154 us -> 152 us (0.987)
  waiting for transfers between devices: 41.8 us -> 40.2 us
    ppermute x11, starting transfers between devices: 28.4 us -> 25.9 us  [shift(): lax.ppermute(value, axis, [(source, source + steps) for source in range(f...]
    unnamed x39 -> x41, local copies, waits for them, and re-layouts: 8.08 us -> 9.11 us
    pallas_call x2 -> x3, Pallas kernels: 25.4 us -> 25.7 us  [the longest x1 15.7 us: second_call(): call(second_kernel, SLOTS // GROUP, [SCALARS] + [ANYWHERE] * 11 + [WHOLE]...]
where the time goes in v2:
time: 152 us
  starting transfers between devices  43.8 us (29%)
  waiting for transfers between devices  40.2 us (26%)
  Pallas kernels  36.6 us (24%)
  local copies, waits for them, and re-layouts  14.6 us (10%)
  blocking collectives  13.6 us (9%)
  between operations  1.59 us (1%)
    ppermute x11, starting transfers between devices, shift(): lax.ppermute(value, axis, [(source, source + steps) for source in range(f...  25.9 us
    pallas_call x1, Pallas kernels, second_call(): call(second_kernel, SLOTS // GROUP, [SCALARS] + [ANYWHERE] * 11 + [WHOLE]...  15.7 us
    ppermute x11, waiting for transfers between devices, shift(): lax.ppermute(value, axis, [(source, source + steps) for source in range(f...  14.3 us
    all_to_all x1, blocking collectives, hand_out(): return lax.all_to_all(spread, axis, 0, 0, tiled=True)  13.6 us
    all_to_all x1, starting transfers between devices, add_shares(): return lax.all_to_all(shares, axis, 0, 0, tiled=True).sum(axis=0)  13.5 us
    pallas_call x2, Pallas kernels, first_call(): call(functools.partial(first_kernel, start), 1, [SCALARS] + [ANYWHERE] *...  10.1 us
    unnamed x41, local copies, waits for them, and re-layouts  9.11 us
    ppermute x1, waiting for transfers between devices, ring_sum(): first = lax.ppermute(value, 'row', pairs)  5.56 us
  transfers between devices with their start and end apart: 18, of which 11 were waited for; matrix products, arithmetic and copies ran while one was open for 2% of the time, Pallas kernels for 13%

profile of v2, /device:TPU:6, one launch (start us, length us, event | category | flops | bytes accessed | tf_op | source)
XLA Modules:
  0.0 151.7 jit_solution(13540605191000317688)
XLA Ops:
  0.6 0.0 copy-start.13
  0.6 2.0 %slice.23 = f32[2,256,256]{2,1,0:T(8,128)} slice(f32[4,256,512]{2,1,0:T(8,128)} %own.4), slice={[0:2], [0:256], [0:256]} | slice | bytes 1048576 | tf_op jit(solution)/shard_map/slice | solution.py:574
  2.7 5.2 %collective-permute-start.1 = (f32[2,256,256]{2,1,0:T(8,128)}, f32[2,256,256]{2,1,0:T(8,128)S(1)}, u32[]{:S(2)}, u32[]{:S(2)}) collective-permute-start(f32[2,256,256]{2,1,0:T(8,128)} %slice.23), channel_id=1, source_target_pairs={{8,0},{16,8},{24,16},{32,24},{40,32},{48,40},{56,48},{64,56},{72,6... | collective-permute-start | bytes 1572872 | tf_op jit(solution)/shard_map/ppermute | solution.py:539
  7.8 2.3 %slice.24 = f32[4,256,256]{2,1,0:T(8,128)} slice(f32[4,256,512]{2,1,0:T(8,128)} %own.4), slice={[0:4], [0:256], [0:256]} | slice | bytes 2097152 | tf_op jit(solution)/shard_map/slice | solution.py:577
  10.1 1.4 collective-permute-start
  11.6 0.0 copy-done.13
  11.6 1.2 fusion
  12.7 2.6 %collective-permute-start.3 = (f32[2,256,256]{2,1,0:T(8,128)}, f32[2,256,256]{2,1,0:T(8,128)S(1)}, u32[]{:S(2)}, u32[]{:S(2)}) collective-permute-start(f32[2,256,256]{2,1,0:T(8,128)} %get-tuple-element.68), channel_id=1, source_target_pairs={{8,0},{16,8},{24,16},{32,24},{40,32},{48,40},{56,48},{64,56},{72,6... | collective-permute-start | bytes 1572872 | tf_op jit(solution)/shard_map/ppermute | solution.py:539
  16.0 0.0 copy-done.16
  16.1 0.1 pad_add_fusion.meta
  16.1 1.0 copy-done.5
  17.2 3.7 %shard_map.95 = (f32[8,256,256]{2,1,0:T(8,128)S(1)}, f32[8,2,256,256]{3,2,1,0:T(8,128)S(1)}) custom-call(s32[17]{0:T(128)S(1)} %pad_add_fusion.meta, f32[2,256,256]{2,1,0:T(8,128)S(1)} %copy-done.5, f32[8,256,256]{2,1,0:T(8,128)S(1)} %copy-done.4, bf16[2,256,256]{2,1,0:T(8,128)(2,1)S(1)} %copy-done.6), custom_call_target="tpu_custom_call" | custom-call | tf_op jit(solution)/shard_map/pallas_call | solution.py:448
  20.9 0.0 copy-start
  20.9 2.0 %copy-done = f32[8,2,256,256]{3,2,1,0:T(8,128)} copy-done((f32[8,2,256,256]{3,2,1,0:T(8,128)}, f32[8,2,256,256]{3,2,1,0:T(8,128)S(1)}, u32[]{:S(2)}) %copy-start) | copy-done | bytes 4194328
  22.9 1.3 copy-done.9
  24.2 0.0 collective-permute-done.1.down0.down0_one
  24.2 1.3 collective-permute-start.4
  25.5 2.7 %collective-permute-start.2 = (f32[2,256,256]{2,1,0:T(8,128)S(1)}, f32[2,256,256]{2,1,0:T(8,128)S(1)}, u32[]{:S(2)}, u32[]{:S(2)}) collective-permute-start(f32[2,256,256]{2,1,0:T(8,128)S(1)} %copy-done.15), channel_id=1, source_target_pairs={{8,0},{16,8},{24,16},{32,24},{40,32},{48,40},{56,48},{64,56},{72,6... | collective-permute-start | bytes 1572872 | tf_op jit(solution)/shard_map/ppermute | solution.py:539
  28.2 0.0 copy-done.14
  28.2 2.1 %collective-permute-start.5 = (f32[2,256,256]{2,1,0:T(8,128)S(1)}, f32[2,256,256]{2,1,0:T(8,128)S(1)}, u32[]{:S(2)}, u32[]{:S(2)}) collective-permute-start(f32[2,256,256]{2,1,0:T(8,128)S(1)} %copy-done.14), channel_id=1, source_target_pairs={{8,0},{16,8},{24,16},{32,24},{40,32},{48,40},{56,48},{64,56},{72,6... | collective-permute-start | bytes 1572872 | tf_op jit(solution)/shard_map/ppermute | solution.py:539
  30.2 1.2 collective-permute-done.3.down1.down1_one
  31.5 0.0 collective-permute-done.right
  31.5 0.0 collective-permute-done.4.corner.corner_one
  31.5 8.0 %shard_map.96.prop_now = f32[4,2,256,256]{3,2,1,0:T(8,128)} custom-call(s32[17]{0:T(128)S(1)} %pad_add_fusion.meta, f32[4,256,512]{2,1,0:T(8,128)} %own.4, f32[4,256,256]{2,1,0:T(8,128)} %collective-permute-done.right, f32[2,256,256]{2,1,0:T(8,128)S(1)} %collective-permute-done.1.down0.down0_one, f32[2,256,256]{2,1,0:T(8,128)S(1)} %collective-permute-done.3.down1.down1_one, ...), custom_call_target="tpu_custom_call" | custom-call | flops 3221225472 | bytes 3145728 | tf_op jit(solution)/shard_map/pallas_call | solution.py:464
  39.5 3.1 %collective-permute-done.2.down0_two = f32[2,256,256]{2,1,0:T(8,128)S(1)} collective-permute-done((f32[2,256,256]{2,1,0:T(8,128)S(1)}, f32[2,256,256]{2,1,0:T(8,128)S(1)}, u32[]{:S(2)}, u32[]{:S(2)}) %collective-permute-start.2) | collective-permute-done | bytes 524320 | tf_op jit(solution)/shard_map/ppermute | solution.py:539
  42.6 1.3 collective-permute-start.6
  44.0 2.1 %shard_map.97.prop_later = f32[4,2,256,256]{3,2,1,0:T(8,128)} custom-call(s32[17]{0:T(128)S(1)} %pad_add_fusion.meta, f32[4,256,512]{2,1,0:T(8,128)} %own.4, f32[4,256,256]{2,1,0:T(8,128)} %collective-permute-done.right, f32[2,256,256]{2,1,0:T(8,128)S(1)} %collective-permute-done.1.down0.down0_one, ...), custom_call_target="tpu_custom_call" | custom-call | tf_op jit(solution)/shard_map/pallas_call | solution.py:464
  46.1 6.9 %collective-permute-done.5.down1_two = f32[2,256,256]{2,1,0:T(8,128)S(1)} collective-permute-done((f32[2,256,256]{2,1,0:T(8,128)S(1)}, f32[2,256,256]{2,1,0:T(8,128)S(1)}, u32[]{:S(2)}, u32[]{:S(2)}) %collective-permute-start.5) | collective-permute-done | bytes 524320 | tf_op jit(solution)/shard_map/ppermute | solution.py:539
  53.0 0.0 collective-permute-done.6.corner_two
  53.0 0.8 copy-done.18
  53.8 0.2 copy-done.19
  54.0 15.7 %shard_map.98 = (f32[2,256,256]{2,1,0:T(8,128)}, f32[8,4,256,256]{3,2,1,0:T(8,128)}) custom-call(s32[17]{0:T(128)} %copy-done.7, f32[4,256,512]{2,1,0:T(8,128)} %own.4, f32[4,256,256]{2,1,0:T(8,128)} %collective-permute-done.right, f32[2,256,256]{2,1,0:T(8,128)} %copy-done.1, f32[2,256,256]{2,1,0:T(8,128)} %copy-done.17, f32[2,256,256]{2,1,0:T(8,128)} %copy-done.2, ...), custom_call_target="tpu_custom_call" | custom-call | flops 12884901888 | bytes 12582912 | tf_op jit(solution)/shard_map/pallas_call | solution.py:483
  69.6 13.5 %all-to-all-start = ((f32[8,64,256]{2,1,0:T(8,128)}), f32[8,64,256]{2,1,0:T(8,128)}, u32[]{:S(2)}, u32[]{:S(2)}) async-start(f32[8,64,256]{2,1,0:T(8,128)} %bitcast.7), calls=%async_computation | async-start | bytes 1048576 | tf_op jit(solution)/shard_map/all_to_all | solution.py:545
  83.1 5.3 %shard_map.99 = (f32[4,256,512]{2,1,0:T(8,128)S(1)}, f32[4,256,256]{2,1,0:T(8,128)S(1)}, f32[4,256,256]{2,1,0:T(8,128)S(1)}, f32[4,256,256]{2,1,0:T(8,128)S(1)}, f32[4,256,256]{2,1,0:T(8,128)S(1)}) custom-call(s32[17]{0:T(128)S(1)} %copy-done.8, f32[8,4,256,256]{3,2,1,0:T(8,128)} %get-tuple-element.52.grads), custom_call_target="tpu_custom_call" | custom-call | flops 6442450944 | bytes 6291456 | tf_op jit(solution)/shard_map/pallas_call | solution.py:504
  88.5 0.0 copy-start.10
  88.5 1.0 copy-done.10
  89.4 1.0 copy-done.11
  90.4 1.0 copy-done.12
  91.4 2.2 %all-to-all-done = f32[8,64,256]{2,1,0:T(8,128)} async-done(((f32[8,64,256]{2,1,0:T(8,128)}), f32[8,64,256]{2,1,0:T(8,128)}, u32[]{:S(2)}, u32[]{:S(2)}) %all-to-all-start) | async-done | bytes 524320 | tf_op jit(solution)/shard_map/all_to_all | solution.py:545
  93.6 1.1 reduce_sum.9
  94.7 1.6 %collective-permute-start.15 = (f32[4,256,256]{2,1,0:T(8,128)}, f32[4,256,256]{2,1,0:T(8,128)S(1)}, u32[]{:S(2)}, u32[]{:S(2)}) collective-permute-start(f32[4,256,256]{2,1,0:T(8,128)} %copy-done.12), channel_id=1, source_target_pairs={{0,1},{1,2},{2,3},{3,4},{4,5},{5,6},{6,7},{8,9},{9,10},{10,11},{11... | collective-permute-start | bytes 3145736 | tf_op jit(solution)/shard_map/ppermute | solution.py:539
  96.3 3.2 %collective-permute-start.13 = (f32[4,256,256]{2,1,0:T(8,128)}, f32[4,256,256]{2,1,0:T(8,128)S(1)}, u32[]{:S(2)}, u32[]{:S(2)}) collective-permute-start(f32[4,256,256]{2,1,0:T(8,128)} %copy-done.11), channel_id=1, source_target_pairs={{0,8},{8,16},{16,24},{24,32},{32,40},{40,48},{48,56},{56,64},{64,7... | collective-permute-start | bytes 3145736 | tf_op jit(solution)/shard_map/ppermute | solution.py:539
  99.5 2.7 %collective-permute-start.7 = (f32[4,256,256]{2,1,0:T(8,128)}, f32[4,256,256]{2,1,0:T(8,128)S(1)}, u32[]{:S(2)}, u32[]{:S(2)}) collective-permute-start(f32[4,256,256]{2,1,0:T(8,128)} %copy-done.10), channel_id=1, source_target_pairs={{0,1},{1,2},{2,3},{3,4},{4,5},{5,6},{6,7},{8,9},{9,10},{10,11},{11... | collective-permute-start | bytes 3145736 | tf_op jit(solution)/shard_map/ppermute | solution.py:539
  102.2 0.6 collective-permute-start.8
  102.8 5.6 %collective-permute-done.8 = f32[64,256]{1,0:T(8,128)S(1)} collective-permute-done((f32[64,256]{1,0:T(8,128)S(1)}, f32[64,256]{1,0:T(8,128)S(1)}, u32[]{:S(2)}, u32[]{:S(2)}) %collective-permute-start.8) | collective-permute-done | bytes 65568 | tf_op jit(solution)/shard_map/ppermute | solution.py:554
  108.4 0.0 collective-permute-start.9
  108.4 5.5 %collective-permute-done.9 = f32[64,256]{1,0:T(8,128)S(1)} collective-permute-done((f32[64,256]{1,0:T(8,128)S(1)}, f32[64,256]{1,0:T(8,128)S(1)}, u32[]{:S(2)}, u32[]{:S(2)}) %collective-permute-start.9) | collective-permute-done | bytes 65568 | tf_op jit(solution)/shard_map/ppermute | solution.py:555
  113.8 0.0 collective-permute-start.10
  113.8 0.0 collective-permute-done.15
  113.8 0.1 add.27
  114.0 1.9 %collective-permute-start.16 = (f32[4,256,256]{2,1,0:T(8,128)S(1)}, f32[4,256,256]{2,1,0:T(8,128)S(1)}, u32[]{:S(2)}, u32[]{:S(2)}) collective-permute-start(f32[4,256,256]{2,1,0:T(8,128)S(1)} %add.27), channel_id=1, source_target_pairs={{0,8},{8,16},{16,24},{24,32},{32,40},{40,48},{48,56},{56,64},{64,7... | collective-permute-start | bytes 3145736 | tf_op jit(solution)/shard_map/ppermute | solution.py:539
  115.9 3.4 %collective-permute-done.10 = f32[64,256]{1,0:T(8,128)S(1)} collective-permute-done((f32[64,256]{1,0:T(8,128)S(1)}, f32[64,256]{1,0:T(8,128)S(1)}, u32[]{:S(2)}, u32[]{:S(2)}) %collective-permute-start.10) | collective-permute-done | bytes 65568 | tf_op jit(solution)/shard_map/ppermute | solution.py:556
  119.3 0.1 collective-permute-start.11
  119.4 4.3 %collective-permute-done.11 = f32[64,256]{1,0:T(8,128)S(1)} collective-permute-done((f32[64,256]{1,0:T(8,128)S(1)}, f32[64,256]{1,0:T(8,128)S(1)}, u32[]{:S(2)}, u32[]{:S(2)}) %collective-permute-start.11) | collective-permute-done | bytes 65568 | tf_op jit(solution)/shard_map/ppermute | solution.py:561
  123.7 1.2 collective-permute-start.12
  124.9 3.0 %collective-permute-done.12 = f32[64,256]{1,0:T(8,128)S(1)} collective-permute-done((f32[64,256]{1,0:T(8,128)S(1)}, f32[64,256]{1,0:T(8,128)S(1)}, u32[]{:S(2)}, u32[]{:S(2)}) %collective-permute-start.12) | collective-permute-done | bytes 65568 | tf_op jit(solution)/shard_map/ppermute | solution.py:562
  127.9 0.0 collective-permute-done.13.down1
  127.9 2.4 %collective-permute-start.14 = (f32[64,256]{1,0:T(8,128)S(1)}, f32[64,256]{1,0:T(8,128)S(1)}, u32[]{:S(2)}, u32[]{:S(2)}) collective-permute-start(f32[64,256]{1,0:T(8,128)S(1)} %collective-permute-done.12), channel_id=1, source_target_pairs={{0,24},{8,0},{16,8},{24,16},{32,56},{40,32},{48,40},{56,48},{64,88... | collective-permute-start | bytes 196616 | tf_op jit(solution)/shard_map/ppermute | solution.py:564
  130.4 1.9 %collective-permute-done.14 = f32[64,256]{1,0:T(8,128)S(1)} collective-permute-done((f32[64,256]{1,0:T(8,128)S(1)}, f32[64,256]{1,0:T(8,128)S(1)}, u32[]{:S(2)}, u32[]{:S(2)}) %collective-permute-start.14) | collective-permute-done | bytes 65568 | tf_op jit(solution)/shard_map/ppermute | solution.py:564
  132.3 0.0 collective-permute-done.7.right
  132.3 13.6 %all_to_all.10 = f32[8,64,256]{2,1,0:T(8,128)S(1)} all-to-all(f32[8,64,256]{2,1,0:T(8,128)S(1)} %broadcast_in_dim.2), channel_id=1, replica_groups=mesh['row'=16,'col'=8] {'col'}, dimensions={0} | all-to-all | bytes 1048576 | tf_op jit(solution)/shard_map/all_to_all | solution.py:550
  145.9 3.1 %collective-permute-done.16.down0 = f32[4,256,256]{2,1,0:T(8,128)S(1)} collective-permute-done((f32[4,256,256]{2,1,0:T(8,128)S(1)}, f32[4,256,256]{2,1,0:T(8,128)S(1)}, u32[]{:S(2)}, u32[]{:S(2)}) %collective-permute-start.16) | collective-permute-done | bytes 1048608 | tf_op jit(solution)/shard_map/ppermute | solution.py:539
  149.0 1.9 %shard_map.100 = f32[4,256,512]{2,1,0:T(8,128)} custom-call(f32[4,256,512]{2,1,0:T(8,128)S(1)} %get-tuple-element.53.base, f32[4,256,256]{2,1,0:T(8,128)S(1)} %collective-permute-done.7.right, f32[4,256,256]{2,1,0:T(8,128)S(1)} %collective-permute-done.16.down0, f32[4,256,256]{2,1,0:T(8,128)S(1)} %collective-permute-done.13.down1), custom_call_target="tpu_custom_call" | custom-call | flops 1048576 | bytes 7340032 | tf_op jit(solution)/shard_map/pallas_call | solution.py:525
  150.9 0.8 copy.12
  (30 shorter events, 0.1 us)
Async XLA Ops:
  0.6 10.9 %copy-start.13 = (f32[4,256,512]{2,1,0:T(8,128)S(1)}, f32[4,256,512]{2,1,0:T(8,128)}, u32[]{:S(2)}) copy-start(f32[4,256,512]{2,1,0:T(8,128)} %own.4) | copy-start | bytes 6291460
  2.7 21.5 %collective-permute-start.1 = (f32[2,256,256]{2,1,0:T(8,128)}, f32[2,256,256]{2,1,0:T(8,128)S(1)}, u32[]{:S(2)}, u32[]{:S(2)}) collective-permute-start(f32[2,256,256]{2,1,0:T(8,128)} %slice.23), channel_id=1, source_target_pairs={{8,0},{16,8},{24,16},{32,24},{40,32},{48,40},{56,48},{64,56},{72,6... | collective-permute-start | bytes 1572872 | tf_op jit(solution)/shard_map/ppermute | solution.py:539
  10.1 5.9 %copy-start.16 = (s32[8,2]{0,1:T(2,128)S(1)}, s32[8,2]{0,1:T(2,128)}, u32[]{:S(2)}) copy-start(s32[8,2]{0,1:T(2,128)} %param.10) | copy-start | bytes 196
  10.1 6.0 %copy-start.4 = (f32[8,256,256]{2,1,0:T(8,128)S(1)}, f32[8,256,256]{2,1,0:T(8,128)}, u32[]{:S(2)}) copy-start(f32[8,256,256]{2,1,0:T(8,128)} %amp.1) | copy-start | bytes 6291460
  10.1 6.0 %copy-start.6 = (bf16[2,256,256]{2,1,0:T(8,128)(2,1)S(1)}, bf16[2,256,256]{2,1,0:T(8,128)(2,1)}, u32[]{:S(2)}) copy-start(bf16[2,256,256]{2,1,0:T(8,128)(2,1)} %constant.23.clone.fold) | copy-start | bytes 786436
  10.1 21.4 %collective-permute-start = (f32[4,256,256]{2,1,0:T(8,128)}, f32[4,256,256]{2,1,0:T(8,128)}, u32[]{:S(2)}, u32[]{:S(2)}) collective-permute-start(f32[4,256,256]{2,1,0:T(8,128)} %slice.24), channel_id=1, source_target_pairs={{1,0},{2,1},{3,2},{4,3},{5,4},{6,5},{7,6},{9,8},{10,9},{11,10},{12... | collective-permute-start | bytes 3145736 | tf_op jit(solution)/shard_map/ppermute | solution.py:539
  12.7 18.8 %collective-permute-start.3 = (f32[2,256,256]{2,1,0:T(8,128)}, f32[2,256,256]{2,1,0:T(8,128)S(1)}, u32[]{:S(2)}, u32[]{:S(2)}) collective-permute-start(f32[2,256,256]{2,1,0:T(8,128)} %get-tuple-element.68), channel_id=1, source_target_pairs={{8,0},{16,8},{24,16},{32,24},{40,32},{48,40},{56,48},{64,56},{72,6... | collective-permute-start | bytes 1572872 | tf_op jit(solution)/shard_map/ppermute | solution.py:539
  16.1 1.0 copy-start.5
  17.2 26.7 %copy-start.7 = (s32[17]{0:T(128)}, s32[17]{0:T(128)S(1)}, u32[]{:S(2)}) copy-start(s32[17]{0:T(128)S(1)} %pad_add_fusion.meta) | copy-start | bytes 208
  17.2 8.3 %copy-start.15 = (f32[2,256,256]{2,1,0:T(8,128)S(1)}, f32[2,256,256]{2,1,0:T(8,128)}, u32[]{:S(2)}) copy-start(f32[2,256,256]{2,1,0:T(8,128)} %get-tuple-element.69) | copy-start | bytes 1572868
  17.2 11.0 %copy-start.14 = (f32[2,256,256]{2,1,0:T(8,128)S(1)}, f32[2,256,256]{2,1,0:T(8,128)}, u32[]{:S(2)}) copy-start(f32[2,256,256]{2,1,0:T(8,128)} %get-tuple-element.51) | copy-start | bytes 1572868
  20.9 2.0 %copy-start = (f32[8,2,256,256]{3,2,1,0:T(8,128)}, f32[8,2,256,256]{3,2,1,0:T(8,128)S(1)}, u32[]{:S(2)}) copy-start(f32[8,2,256,256]{3,2,1,0:T(8,128)S(1)} %get-tuple-element.48.turned_in) | copy-start | bytes 12582916
  22.9 1.3 copy-start.9
  24.2 19.7 %copy-start.1 = (f32[2,256,256]{2,1,0:T(8,128)}, f32[2,256,256]{2,1,0:T(8,128)S(1)}, u32[]{:S(2)}) copy-start(f32[2,256,256]{2,1,0:T(8,128)S(1)} %collective-permute-done.1.down0.down0_one) | copy-start | bytes 1572868
  24.2 7.3 %collective-permute-start.4 = (f32[2,256,256]{2,1,0:T(8,128)S(1)}, f32[2,256,256]{2,1,0:T(8,128)S(1)}, u32[]{:S(2)}, u32[]{:S(2)}) collective-permute-start(f32[2,256,256]{2,1,0:T(8,128)S(1)} %collective-permute-done.1.down0.down0_one), channel_id=1, source_target_pairs={{1,0},{2,1},{3,2},{4,3},{5,4},{6,5},{7,6},{9,8},{10,9},{11,10},{12... | collective-permute-start | bytes 1572872 | tf_op jit(solution)/shard_map/ppermute | solution.py:539
  25.5 17.1 %collective-permute-start.2 = (f32[2,256,256]{2,1,0:T(8,128)S(1)}, f32[2,256,256]{2,1,0:T(8,128)S(1)}, u32[]{:S(2)}, u32[]{:S(2)}) collective-permute-start(f32[2,256,256]{2,1,0:T(8,128)S(1)} %copy-done.15), channel_id=1, source_target_pairs={{8,0},{16,8},{24,16},{32,24},{40,32},{48,40},{56,48},{64,56},{72,6... | collective-permute-start | bytes 1572872 | tf_op jit(solution)/shard_map/ppermute | solution.py:539
  28.2 24.8 %collective-permute-start.5 = (f32[2,256,256]{2,1,0:T(8,128)S(1)}, f32[2,256,256]{2,1,0:T(8,128)S(1)}, u32[]{:S(2)}, u32[]{:S(2)}) collective-permute-start(f32[2,256,256]{2,1,0:T(8,128)S(1)} %copy-done.14), channel_id=1, source_target_pairs={{8,0},{16,8},{24,16},{32,24},{40,32},{48,40},{56,48},{64,56},{72,6... | collective-permute-start | bytes 1572872 | tf_op jit(solution)/shard_map/ppermute | solution.py:539
  31.5 12.4 %copy-start.2 = (f32[2,256,256]{2,1,0:T(8,128)}, f32[2,256,256]{2,1,0:T(8,128)S(1)}, u32[]{:S(2)}) copy-start(f32[2,256,256]{2,1,0:T(8,128)S(1)} %collective-permute-done.3.down1.down1_one) | copy-start | bytes 1572868
  31.5 12.4 %copy-start.3 = (f32[2,256,256]{2,1,0:T(8,128)}, f32[2,256,256]{2,1,0:T(8,128)S(1)}, u32[]{:S(2)}) copy-start(f32[2,256,256]{2,1,0:T(8,128)S(1)} %collective-permute-done.4.corner.corner_one) | copy-start | bytes 1572868
  42.6 3.4 %copy-start.17 = (f32[2,256,256]{2,1,0:T(8,128)}, f32[2,256,256]{2,1,0:T(8,128)S(1)}, u32[]{:S(2)}) copy-start(f32[2,256,256]{2,1,0:T(8,128)S(1)} %collective-permute-done.2.down0_two) | copy-start | bytes 1572868
  42.6 10.3 %collective-permute-start.6 = (f32[2,256,256]{2,1,0:T(8,128)S(1)}, f32[2,256,256]{2,1,0:T(8,128)S(1)}, u32[]{:S(2)}, u32[]{:S(2)}) collective-permute-start(f32[2,256,256]{2,1,0:T(8,128)S(1)} %collective-permute-done.2.down0_two), channel_id=1, source_target_pairs={{1,0},{2,1},{3,2},{4,3},{5,4},{6,5},{7,6},{9,8},{10,9},{11,10},{12... | collective-permute-start | bytes 1572872 | tf_op jit(solution)/shard_map/ppermute | solution.py:539
  53.0 0.8 copy-start.18
  53.0 1.0 copy-start.19
  54.0 29.2 %copy-start.8 = (s32[17]{0:T(128)S(1)}, s32[17]{0:T(128)}, u32[]{:S(2)}) copy-start(s32[17]{0:T(128)} %copy-done.7) | copy-start | bytes 208
  69.6 23.9 %all-to-all-start = ((f32[8,64,256]{2,1,0:T(8,128)}), f32[8,64,256]{2,1,0:T(8,128)}, u32[]{:S(2)}, u32[]{:S(2)}) async-start(f32[8,64,256]{2,1,0:T(8,128)} %bitcast.7), calls=%async_computation | async-start | bytes 1048576 | tf_op jit(solution)/shard_map/all_to_all | solution.py:545
  88.5 1.0 copy-start.10
  89.4 1.0 copy-start.11
  90.4 1.0 copy-start.12
  94.7 19.2 %collective-permute-start.15 = (f32[4,256,256]{2,1,0:T(8,128)}, f32[4,256,256]{2,1,0:T(8,128)S(1)}, u32[]{:S(2)}, u32[]{:S(2)}) collective-permute-start(f32[4,256,256]{2,1,0:T(8,128)} %copy-done.12), channel_id=1, source_target_pairs={{0,1},{1,2},{2,3},{3,4},{4,5},{5,6},{6,7},{8,9},{9,10},{10,11},{11... | collective-permute-start | bytes 3145736 | tf_op jit(solution)/shard_map/ppermute | solution.py:539
  96.3 31.7 %collective-permute-start.13 = (f32[4,256,256]{2,1,0:T(8,128)}, f32[4,256,256]{2,1,0:T(8,128)S(1)}, u32[]{:S(2)}, u32[]{:S(2)}) collective-permute-start(f32[4,256,256]{2,1,0:T(8,128)} %copy-done.11), channel_id=1, source_target_pairs={{0,8},{8,16},{16,24},{24,32},{32,40},{40,48},{48,56},{56,64},{64,7... | collective-permute-start | bytes 3145736 | tf_op jit(solution)/shard_map/ppermute | solution.py:539
  99.5 32.8 %collective-permute-start.7 = (f32[4,256,256]{2,1,0:T(8,128)}, f32[4,256,256]{2,1,0:T(8,128)S(1)}, u32[]{:S(2)}, u32[]{:S(2)}) collective-permute-start(f32[4,256,256]{2,1,0:T(8,128)} %copy-done.10), channel_id=1, source_target_pairs={{0,1},{1,2},{2,3},{3,4},{4,5},{5,6},{6,7},{8,9},{9,10},{10,11},{11... | collective-permute-start | bytes 3145736 | tf_op jit(solution)/shard_map/ppermute | solution.py:539
  102.2 6.2 %collective-permute-start.8 = (f32[64,256]{1,0:T(8,128)S(1)}, f32[64,256]{1,0:T(8,128)S(1)}, u32[]{:S(2)}, u32[]{:S(2)}) collective-permute-start(f32[64,256]{1,0:T(8,128)S(1)} %reduce_sum.9), channel_id=1, source_target_pairs={{0,96},{8,104},{16,112},{24,120},{32,0},{40,8},{48,16},{56,24},{64... | collective-permute-start | bytes 196616 | tf_op jit(solution)/shard_map/ppermute | solution.py:554
  108.4 5.5 %collective-permute-start.9 = (f32[64,256]{1,0:T(8,128)S(1)}, f32[64,256]{1,0:T(8,128)S(1)}, u32[]{:S(2)}, u32[]{:S(2)}) collective-permute-start(f32[64,256]{1,0:T(8,128)S(1)} %collective-permute-done.8), channel_id=1, source_target_pairs={{0,96},{8,104},{16,112},{24,120},{32,0},{40,8},{48,16},{56,24},{64... | collective-permute-start | bytes 196616 | tf_op jit(solution)/shard_map/ppermute | solution.py:555
  113.8 5.5 %collective-permute-start.10 = (f32[64,256]{1,0:T(8,128)S(1)}, f32[64,256]{1,0:T(8,128)S(1)}, u32[]{:S(2)}, u32[]{:S(2)}) collective-permute-start(f32[64,256]{1,0:T(8,128)S(1)} %collective-permute-done.9), channel_id=1, source_target_pairs={{0,96},{8,104},{16,112},{24,120},{32,0},{40,8},{48,16},{56,24},{64... | collective-permute-start | bytes 196616 | tf_op jit(solution)/shard_map/ppermute | solution.py:556
  114.0 35.0 %collective-permute-start.16 = (f32[4,256,256]{2,1,0:T(8,128)S(1)}, f32[4,256,256]{2,1,0:T(8,128)S(1)}, u32[]{:S(2)}, u32[]{:S(2)}) collective-permute-start(f32[4,256,256]{2,1,0:T(8,128)S(1)} %add.27), channel_id=1, source_target_pairs={{0,8},{8,16},{16,24},{24,32},{32,40},{40,48},{48,56},{56,64},{64,7... | collective-permute-start | bytes 3145736 | tf_op jit(solution)/shard_map/ppermute | solution.py:539
  119.3 4.3 %collective-permute-start.11 = (f32[64,256]{1,0:T(8,128)S(1)}, f32[64,256]{1,0:T(8,128)S(1)}, u32[]{:S(2)}, u32[]{:S(2)}) collective-permute-start(f32[64,256]{1,0:T(8,128)S(1)} %add_add_fusion.1), channel_id=1, source_target_pairs={{0,24},{8,0},{16,8},{24,16},{32,56},{40,32},{48,40},{56,48},{64,88... | collective-permute-start | bytes 196616 | tf_op jit(solution)/shard_map/ppermute | solution.py:561
  123.7 4.3 %collective-permute-start.12 = (f32[64,256]{1,0:T(8,128)S(1)}, f32[64,256]{1,0:T(8,128)S(1)}, u32[]{:S(2)}, u32[]{:S(2)}) collective-permute-start(f32[64,256]{1,0:T(8,128)S(1)} %collective-permute-done.11), channel_id=1, source_target_pairs={{0,24},{8,0},{16,8},{24,16},{32,56},{40,32},{48,40},{56,48},{64,88... | collective-permute-start | bytes 196616 | tf_op jit(solution)/shard_map/ppermute | solution.py:562
  127.9 4.3 %collective-permute-start.14 = (f32[64,256]{1,0:T(8,128)S(1)}, f32[64,256]{1,0:T(8,128)S(1)}, u32[]{:S(2)}, u32[]{:S(2)}) collective-permute-start(f32[64,256]{1,0:T(8,128)S(1)} %collective-permute-done.12), channel_id=1, source_target_pairs={{0,24},{8,0},{16,8},{24,16},{32,56},{40,32},{48,40},{56,48},{64,88... | collective-permute-start | bytes 196616 | tf_op jit(solution)/shard_map/ppermute | solution.py:564
